TPU v7x, 32 devices: a whole 2x2x4 slice. The times are simulated.
32 devices in a mesh: blk: 4 (over y, core), dp: 8 (over z, x).
Axes of the slice: x: 2, y: 2, z: 4, core: 2. Of those that a mesh axis runs over, the one named last changes fastest.
Arguments:
- inputs: bfloat16 [8, 1024, 512], P('dp', 'blk'), may hold values from -6 to 6
- segments: int32 [8, 1024], P('dp'), may hold values from 0 to 32, as said below
- attention_routes: int32 [2, 8, 1024, 4], P(None, 'dp', 'blk'), may hold values from 0 to 7, all different within a row
- expert_routes: int32 [2, 8, 1024, 2], P(None, 'dp', 'blk'), may hold values from 0 to 15, all different within a row; in each aligned block of 256 rows (0 to 255, 256 to 511, ..., all dimensions but the last counted through in order) at most 48 rows name the same one
- gain_mixer: bfloat16 [512], replicated, may hold values from 0.5 to 1.5
- gain_expert: bfloat16 [512], replicated, may hold values from 0.5 to 1.5
- weight_query: bfloat16 [8, 512, 512], P(None, 'dp', 'blk'), may hold values from -0.25 to 0.25
- weight_key: bfloat16 [512, 512], P('dp', 'blk'), may hold values from -0.25 to 0.25
- weight_value: bfloat16 [512, 512], P('dp', 'blk'), may hold values from -0.25 to 0.25
- weight_out: bfloat16 [8, 512, 512], P(None, 'blk', 'dp'), may hold values from -2 to 2
- router_mixer: bfloat16 [512, 8], replicated, may hold values from -0.125 to 0.125
- router_expert: bfloat16 [512, 16], replicated, may hold values from -0.1875 to 0.1875
- weight_in: bfloat16 [16, 512, 2048], P('dp', 'blk'), may hold values from -0.25 to 0.25
- weight_back: bfloat16 [16, 2048, 512], P('dp', 'blk'), may hold values from -0.125 to 0.125
- halt_weight: bfloat16 [512], replicated, may hold values from -0.25 to 0.25
- cotangent: bfloat16 [8, 1024, 512], P('dp', 'blk'), may hold values from -6 to 6
Outputs:
- result: bfloat16 [8, 1024, 512], P('dp', 'blk')
- input_grad: bfloat16 [8, 1024, 512], P('dp', 'blk')
- gain_mixer_grad: float32 [512], replicated
- gain_expert_grad: float32 [512], replicated
- query_grad: float32 [8, 512, 512], P(None, 'dp', 'blk')
- key_grad: float32 [512, 512], P('dp', 'blk')
- value_grad: float32 [512, 512], P('dp', 'blk')
- out_grad: float32 [8, 512, 512], P(None, 'blk', 'dp')
- router_mixer_grad: float32 [512, 8], replicated
- router_expert_grad: float32 [512, 16], replicated
- in_grad: float32 [16, 512, 2048], P('dp', 'blk')
- back_grad: float32 [16, 2048, 512], P('dp', 'blk')
- halt_grad: float32 [512], replicated
Inputs may be any that keep to these rules, and one draw needn't show every extreme that they name: `segments`: each pack is cut into sentences along its positions: a first one of 1 to b - 1 positions, then sentences of exactly b positions, the last one possibly shorter, where the pack's bucket length b is 256, 128, 64 or 32; pack 0 has b = 256 and the last pack b = 32. No sentence begins at a multiple of 256. Ids number the sentences of a pack from 0 in order. `attention_routes`: each position names 4 different attention experts. `expert_routes`: each position names 2 different experts. In each aligned block of 256 positions of one step and pack, no expert is named by more than 48 positions; some expert is named by exactly 48 in some blocks.
All inputs are finite; a program needn't handle non-finite values.
Results may differ from a plain program's by a relative error of at most 0.024.
Values may be sent and summed in bfloat16 or wider, within the bound.
A program may use at most 256 MiB of HBM per device.

v0:
```python
import jax
import jax.numpy as jnp
from jax import lax
from jax.sharding import PartitionSpec as P

HEADS = 8
HD = 64
MAXLEN = 256


EPSILON = 1e-06
PRECISE = lax.Precision.HIGHEST
MASKED_SCORE = -1e30


def passed_along(value, axis, by):
    length = lax.axis_size(axis)
    pairs = [(i, i + by) for i in range(length) if 0 <= i + by < length]
    return lax.ppermute(value, axis, pairs)


def norm_parts(values_in, gain_vec):
    inverse = lax.rsqrt(jnp.mean(values_in * values_in, axis=-1, keepdims=True) + EPSILON)
    return (inverse, values_in * inverse * gain_vec)


def norm_back(values_in, inverse, gain_vec, grad_out):
    scaled = grad_out * gain_vec
    return inverse * scaled - values_in * (inverse * inverse * inverse) * jnp.mean(
        scaled * values_in, axis=-1, keepdims=True
    )


def gelu_slope(values_in):
    return (
        0.5 * (1.0 + lax.erf(values_in * 0.7071067811865476))
        + values_in * jnp.exp(-0.5 * values_in * values_in) * 0.3989422804014327
    )


def pick_softmax(logits_all, one_hot):
    picked_logits = jnp.sum(one_hot * logits_all[:, :, None, :], axis=-1)
    return jax.nn.softmax(picked_logits, axis=-1)


def softmax_back(weights, grad_in):
    return weights * (grad_in - jnp.sum(weights * grad_in, axis=-1, keepdims=True))


def on_device(
    inputs,
    segments,
    attention_routes,
    expert_routes,
    gain_mixer,
    gain_expert,
    weight_query,
    weight_key,
    weight_value,
    weight_out,
    router_mixer,
    router_expert,
    weight_in,
    weight_back,
    halt_weight,
    cotangent,
):
    rows_dev = inputs.shape[0]
    seq_dev = inputs.shape[1]
    width = inputs.shape[2]
    mixers = weight_query.shape[0]
    top_mixers = attention_routes.shape[-1]
    top_experts = expert_routes.shape[-1]
    expert_local = weight_in.shape[0]
    experts_total = router_expert.shape[1]
    group_size = lax.axis_size("dp")
    capacity = max(2, 3 * seq_dev // experts_total) * rows_dev
    score_scale = HD ** (-0.5)
    feature_count = HEADS * HD
    half_rows = seq_dev // 2
    window = MAXLEN + half_rows
    block_starts = [
        (block_number * half_rows, block_number * half_rows + seq_dev - MAXLEN)
        for block_number in range(2)
    ]
    full_query, full_out, full_key, full_value, local_in, local_back = (
        lax.all_gather(weight_query, "blk", axis=2, tiled=True),
        lax.all_gather(weight_out, "blk", axis=1, tiled=True),
        lax.all_gather(weight_key, "blk", axis=1, tiled=True),
        lax.all_gather(weight_value, "blk", axis=1, tiled=True),
        lax.all_gather(weight_in, "blk", axis=1, tiled=True),
        lax.all_gather(weight_back, "blk", axis=1, tiled=True),
    )
    full_query, full_out, full_key, full_value = (
        lax.all_gather(full_query, "dp", axis=1, tiled=True),
        lax.all_gather(full_out, "dp", axis=2, tiled=True),
        lax.all_gather(full_key, "dp", axis=0, tiled=True),
        lax.all_gather(full_value, "dp", axis=0, tiled=True),
    )
    gain_one = gain_mixer.astype(jnp.float32)
    gain_two = gain_expert.astype(jnp.float32)
    router_one = router_mixer.astype(jnp.float32)
    router_two = router_expert.astype(jnp.float32)
    halt_float = halt_weight.astype(jnp.float32)
    mixer_ids = jnp.arange(mixers, dtype=jnp.int32)
    expert_ids = jnp.arange(experts_total, dtype=jnp.int32)
    offset = lax.axis_index("blk") * seq_dev
    query_pos = offset + jnp.arange(seq_dev, dtype=jnp.int32)
    key_pos = offset - seq_dev + jnp.arange(2 * seq_dev, dtype=jnp.int32)
    own_segment = lax.dynamic_slice_in_dim(segments, offset, seq_dev, 1)
    prior_segment = lax.dynamic_slice_in_dim(segments, jnp.maximum(offset - seq_dev, 0), seq_dev, 1)
    key_segment = jnp.concatenate([prior_segment, own_segment], axis=1)
    allowed = (
        (key_pos[None, None, :] >= 0)
        & (key_pos[None, None, :] <= query_pos[None, :, None])
        & (key_segment[:, None, :] == own_segment[:, :, None])
    )

    def block_scores(query_heads, key_heads, q_start, k_start):
        query_part = query_heads[:, :, q_start : q_start + half_rows]
        key_part = key_heads[:, k_start : k_start + window]
        mask_part = allowed[:, q_start : q_start + half_rows, k_start : k_start + window]
        scores = (
            jnp.einsum(
                "rjshc,rthc->rjhst", query_part, key_part, preferred_element_type=jnp.float32
            )
            * score_scale
        )
        return jnp.where(mask_part[:, None, None], scores, MASKED_SCORE)

    def step_forward(layer_in, turn):
        mixer_pick = attention_routes[turn]
        expert_pick = expert_routes[turn]
        inverse_one, normed_pre = norm_parts(layer_in, gain_one)
        normed = normed_pre.astype(jnp.bfloat16)
        own_keys = jnp.dot(normed, full_key, preferred_element_type=jnp.float32).astype(
            jnp.bfloat16
        )
        own_values = jnp.dot(normed, full_value, preferred_element_type=jnp.float32).astype(
            jnp.bfloat16
        )
        prior_keys, prior_values = passed_along((own_keys, own_values), "blk", 1)
        key_heads = jnp.concatenate([prior_keys, own_keys], axis=1).reshape(
            rows_dev, 2 * seq_dev, HEADS, HD
        )
        value_heads = jnp.concatenate([prior_values, own_values], axis=1).reshape(
            rows_dev, 2 * seq_dev, HEADS, HD
        )
        mixer_logits = jnp.dot(normed, router_mixer, preferred_element_type=jnp.float32)
        mixer_hot = (mixer_pick[..., None] == mixer_ids).astype(jnp.float32)
        mixer_gates = pick_softmax(mixer_logits, mixer_hot)
        every_query = jnp.einsum(
            "rsd,edc->ersc", normed, full_query, preferred_element_type=jnp.float32
        ).astype(jnp.bfloat16)
        query_heads = jnp.einsum(
            "rsje,ersc->rjsc",
            mixer_hot.astype(jnp.bfloat16),
            every_query,
            preferred_element_type=jnp.float32,
        ).astype(jnp.bfloat16)
        query_heads = query_heads.reshape(rows_dev, top_mixers, seq_dev, HEADS, HD)
        attended_parts = []
        log_parts = []
        for q_start, k_start in block_starts:
            scores = block_scores(query_heads, key_heads, q_start, k_start)
            top_score = jnp.max(scores, axis=-1, keepdims=True)
            exp_scores = jnp.exp(scores - top_score)
            score_total = jnp.sum(exp_scores, axis=-1, keepdims=True)
            log_parts.append(top_score + jnp.log(score_total))
            probs_low = (exp_scores / score_total).astype(jnp.bfloat16)
            attended_parts.append(
                jnp.einsum(
                    "rjhst,rthc->rjshc",
                    probs_low,
                    value_heads[:, k_start : k_start + window],
                    preferred_element_type=jnp.float32,
                )
            )
        attended = jnp.concatenate(attended_parts, axis=2).reshape(
            rows_dev, top_mixers, seq_dev, feature_count
        )
        mixer_coeff = mixer_hot * mixer_gates[..., None]
        mixed = jnp.einsum("rsje,rjsc->ersc", mixer_coeff, attended, precision=PRECISE).astype(
            jnp.bfloat16
        )
        middle = layer_in + jnp.einsum(
            "ersc,ecd->rsd", mixed, full_out, preferred_element_type=jnp.float32
        )
        inverse_two, normed_pre_two = norm_parts(middle, gain_two)
        normed_two = normed_pre_two.astype(jnp.bfloat16)
        expert_logits = jnp.dot(normed_two, router_expert, preferred_element_type=jnp.float32)
        expert_hot = (expert_pick[..., None] == expert_ids).astype(jnp.float32)
        expert_gates = pick_softmax(expert_logits, expert_hot)
        flat_pick = expert_pick.reshape(-1)
        member = (flat_pick[:, None] == expert_ids[None, :]).astype(jnp.int32)
        within = jnp.sum(jnp.cumsum(member, axis=0) * member, axis=1) - 1
        slot_index = flat_pick * capacity + within
        copies = jnp.repeat(normed_two.reshape(rows_dev * seq_dev, width), top_experts, axis=0)
        outgoing = (
            jnp.zeros((experts_total * capacity, width), jnp.bfloat16).at[slot_index].set(copies)
        )
        outgoing = outgoing.reshape(group_size, expert_local, capacity, width)
        arrived = lax.all_to_all(outgoing, "dp", split_axis=0, concat_axis=0, tiled=True)
        inner = jnp.einsum("sxcd,xdf->sxcf", arrived, local_in, preferred_element_type=jnp.float32)
        hidden_act = jax.nn.gelu(inner, approximate=False).astype(jnp.bfloat16)
        produced = jnp.einsum(
            "sxcf,xfd->sxcd", hidden_act, local_back, preferred_element_type=jnp.float32
        ).astype(jnp.bfloat16)
        returned = lax.all_to_all(produced, "dp", split_axis=0, concat_axis=0, tiled=True).reshape(
            experts_total * capacity, width
        )
        returned_rows = (
            returned[slot_index].astype(jnp.float32).reshape(rows_dev, seq_dev, top_experts, width)
        )
        layer_out = middle + jnp.sum(expert_gates[..., None] * returned_rows, axis=2)
        saved = dict(
            layer_in=layer_in,
            inverse_one=inverse_one,
            normed=normed,
            key_heads=key_heads,
            value_heads=value_heads,
            mixer_hot=mixer_hot,
            mixer_gates=mixer_gates,
            query_heads=query_heads,
            log_parts=tuple(log_parts),
            attended=attended,
            mixed=mixed,
            middle=middle,
            inverse_two=inverse_two,
            normed_two=normed_two,
            expert_hot=expert_hot,
            expert_gates=expert_gates,
            slot_index=slot_index,
            arrived=arrived,
            inner=inner,
            hidden_act=hidden_act,
            returned_rows=returned_rows,
        )
        return (layer_out, saved)

    def step_backward(grad_out, saved):
        slot_index = saved["slot_index"]
        expert_gates = saved["expert_gates"]
        grad_expert_gates = jnp.sum(grad_out[:, :, None, :] * saved["returned_rows"], axis=-1)
        grad_rows = (expert_gates[..., None] * grad_out[:, :, None, :]).astype(jnp.bfloat16)
        grad_rows = grad_rows.reshape(rows_dev * seq_dev * top_experts, width)
        grad_outgoing = (
            jnp.zeros((experts_total * capacity, width), jnp.bfloat16).at[slot_index].set(grad_rows)
        )
        grad_outgoing = grad_outgoing.reshape(group_size, expert_local, capacity, width)
        grad_produced = lax.all_to_all(grad_outgoing, "dp", split_axis=0, concat_axis=0, tiled=True)
        grad_hidden = jnp.einsum(
            "sxcd,xfd->sxcf", grad_produced, local_back, preferred_element_type=jnp.float32
        )
        grad_inner = (grad_hidden * gelu_slope(saved["inner"])).astype(jnp.bfloat16)
        grad_back_w = jnp.einsum(
            "sxcf,sxcd->xfd", saved["hidden_act"], grad_produced, preferred_element_type=jnp.float32
        )
        grad_in_w = jnp.einsum(
            "sxcd,sxcf->xdf", saved["arrived"], grad_inner, preferred_element_type=jnp.float32
        )
        grad_arrived = jnp.einsum(
            "sxcf,xdf->sxcd", grad_inner, local_in, preferred_element_type=jnp.float32
        ).astype(jnp.bfloat16)
        grad_sent = lax.all_to_all(grad_arrived, "dp", split_axis=0, concat_axis=0, tiled=True)
        grad_sent = grad_sent.reshape(experts_total * capacity, width)
        grad_normed_two = jnp.sum(
            grad_sent[slot_index]
            .astype(jnp.float32)
            .reshape(rows_dev, seq_dev, top_experts, width),
            axis=2,
        )
        grad_expert_pick = softmax_back(expert_gates, grad_expert_gates)
        grad_expert_logits = jnp.sum(saved["expert_hot"] * grad_expert_pick[..., None], axis=2)
        normed_two_f = saved["normed_two"].astype(jnp.float32)
        grad_router_two = jnp.einsum(
            "rsd,rse->de", normed_two_f, grad_expert_logits, precision=PRECISE
        )
        grad_normed_two = grad_normed_two + jnp.einsum(
            "rse,de->rsd", grad_expert_logits, router_two, precision=PRECISE
        )
        middle = saved["middle"]
        inverse_two = saved["inverse_two"]
        grad_gain_two = jnp.sum(grad_normed_two * middle * inverse_two, axis=(0, 1))
        grad_middle = grad_out + norm_back(middle, inverse_two, gain_two, grad_normed_two)
        grad_branch = grad_middle.astype(jnp.bfloat16)
        grad_out_w = jnp.einsum(
            "ersc,rsd->ecd", saved["mixed"], grad_branch, preferred_element_type=jnp.float32
        )
        grad_mixed = jnp.einsum(
            "rsd,ecd->ersc", grad_branch, full_out, preferred_element_type=jnp.float32
        )
        mixer_hot = saved["mixer_hot"]
        mixer_gates = saved["mixer_gates"]
        attended = saved["attended"]
        grad_picked = jnp.einsum("rsje,ersc->rjsc", mixer_hot, grad_mixed, precision=PRECISE)
        grad_mixer_gates = jnp.transpose(jnp.sum(grad_picked * attended, axis=-1), (0, 2, 1))
        grad_attended = (grad_picked * jnp.transpose(mixer_gates, (0, 2, 1))[..., None]).astype(
            jnp.bfloat16
        )
        grad_attended = grad_attended.reshape(rows_dev, top_mixers, seq_dev, HEADS, HD)
        query_heads = saved["query_heads"]
        key_heads = saved["key_heads"]
        value_heads = saved["value_heads"]
        grad_keys_all = jnp.zeros((rows_dev, 2 * seq_dev, HEADS, HD), jnp.float32)
        grad_values_all = jnp.zeros((rows_dev, 2 * seq_dev, HEADS, HD), jnp.float32)
        grad_query_parts = []
        for block_number in range(2):
            q_start, k_start = block_starts[block_number]
            scores = block_scores(query_heads, key_heads, q_start, k_start)
            probs = jnp.exp(scores - saved["log_parts"][block_number])
            grad_att_part = grad_attended[:, :, q_start : q_start + half_rows]
            key_part = key_heads[:, k_start : k_start + window]
            value_part = value_heads[:, k_start : k_start + window]
            grad_values_part = jnp.einsum(
                "rjhst,rjshc->rthc",
                probs.astype(jnp.bfloat16),
                grad_att_part,
                preferred_element_type=jnp.float32,
            )
            grad_probs = jnp.einsum(
                "rjshc,rthc->rjhst", grad_att_part, value_part, preferred_element_type=jnp.float32
            )
            grad_scores = softmax_back(probs, grad_probs).astype(jnp.bfloat16)
            grad_query_parts.append(
                jnp.einsum(
                    "rjhst,rthc->rjshc", grad_scores, key_part, preferred_element_type=jnp.float32
                )
                * score_scale
            )
            grad_keys_part = (
                jnp.einsum(
                    "rjhst,rjshc->rthc",
                    grad_scores,
                    query_heads[:, :, q_start : q_start + half_rows],
                    preferred_element_type=jnp.float32,
                )
                * score_scale
            )
            grad_keys_all = grad_keys_all.at[:, k_start : k_start + window].add(grad_keys_part)
            grad_values_all = grad_values_all.at[:, k_start : k_start + window].add(
                grad_values_part
            )
        grad_queries = jnp.concatenate(grad_query_parts, axis=2)
        grad_keys_all = grad_keys_all.reshape(rows_dev, 2 * seq_dev, feature_count)
        grad_values_all = grad_values_all.reshape(rows_dev, 2 * seq_dev, feature_count)
        next_keys, next_values = (
            passed_along(grad_keys_all[:, :seq_dev].astype(jnp.bfloat16), "blk", -1).astype(
                jnp.float32
            ),
            passed_along(grad_values_all[:, :seq_dev].astype(jnp.bfloat16), "blk", -1).astype(
                jnp.float32
            ),
        )
        grad_keys = (grad_keys_all[:, seq_dev:] + next_keys).astype(jnp.bfloat16)
        grad_values = (grad_values_all[:, seq_dev:] + next_values).astype(jnp.bfloat16)
        grad_every = jnp.einsum(
            "rsje,rjsc->ersc",
            mixer_hot,
            grad_queries.reshape(rows_dev, top_mixers, seq_dev, feature_count),
            precision=PRECISE,
        ).astype(jnp.bfloat16)
        normed = saved["normed"]
        grad_query_w = jnp.einsum(
            "rsd,ersc->edc", normed, grad_every, preferred_element_type=jnp.float32
        )
        grad_key_w = jnp.einsum(
            "rsd,rsc->dc", normed, grad_keys, preferred_element_type=jnp.float32
        )
        grad_value_w = jnp.einsum(
            "rsd,rsc->dc", normed, grad_values, preferred_element_type=jnp.float32
        )
        grad_normed = jnp.einsum(
            "ersc,edc->rsd", grad_every, full_query, preferred_element_type=jnp.float32
        )
        grad_normed = grad_normed + jnp.einsum(
            "rsc,dc->rsd", grad_keys, full_key, preferred_element_type=jnp.float32
        )
        grad_normed = grad_normed + jnp.einsum(
            "rsc,dc->rsd", grad_values, full_value, preferred_element_type=jnp.float32
        )
        grad_mixer_pick = softmax_back(mixer_gates, grad_mixer_gates)
        grad_mixer_logits = jnp.sum(mixer_hot * grad_mixer_pick[..., None], axis=2)
        grad_router_one = jnp.einsum(
            "rsd,rse->de", normed.astype(jnp.float32), grad_mixer_logits, precision=PRECISE
        )
        grad_normed = grad_normed + jnp.einsum(
            "rse,de->rsd", grad_mixer_logits, router_one, precision=PRECISE
        )
        layer_in = saved["layer_in"]
        inverse_one = saved["inverse_one"]
        grad_gain_one = jnp.sum(grad_normed * layer_in * inverse_one, axis=(0, 1))
        grad_layer_in = grad_middle + norm_back(layer_in, inverse_one, gain_one, grad_normed)
        grads_all = (
            grad_gain_one,
            grad_gain_two,
            grad_query_w,
            grad_key_w,
            grad_value_w,
            grad_out_w,
            grad_router_one,
            grad_router_two,
            grad_in_w,
            grad_back_w,
        )
        return (grad_layer_in, grads_all)

    start_state = inputs.astype(jnp.float32)
    first_out, saved_first = step_forward(start_state, 0)
    second_out, saved_second = step_forward(first_out, 1)
    stop_prob = jax.nn.sigmoid(jnp.einsum("rsd,d->rs", first_out, halt_float, precision=PRECISE))[
        ..., None
    ]
    result = (stop_prob * first_out + (1.0 - stop_prob) * second_out).astype(jnp.bfloat16)
    grad_result = cotangent.astype(jnp.float32)
    grad_second = (1.0 - stop_prob) * grad_result
    grad_stop = jnp.sum(grad_result * (first_out - second_out), axis=-1, keepdims=True)
    grad_logit = grad_stop * stop_prob * (1.0 - stop_prob)
    grad_halt = jnp.einsum("rs,rsd->d", grad_logit[..., 0], first_out, precision=PRECISE)
    grad_first = stop_prob * grad_result + grad_logit * halt_float
    grad_first_more, grads_second = step_backward(grad_second, saved_second)
    grad_first = grad_first + grad_first_more
    grad_start, grads_first = step_backward(grad_first, saved_first)
    summed = jax.tree.map(jnp.add, grads_first, grads_second)
    (
        grad_gain_one,
        grad_gain_two,
        grad_query_w,
        grad_key_w,
        grad_value_w,
        grad_out_w,
        grad_router_one,
        grad_router_two,
        grad_in_w,
        grad_back_w,
    ) = summed
    grad_gain_one, grad_gain_two, grad_router_one, grad_router_two, grad_halt = lax.psum(
        (grad_gain_one, grad_gain_two, grad_router_one, grad_router_two, grad_halt), ("blk", "dp")
    )
    grad_query_w, grad_out_w, grad_key_w, grad_value_w = (
        lax.psum_scatter(
            grad_query_w.astype(jnp.bfloat16), "dp", scatter_dimension=1, tiled=True
        ).astype(jnp.float32),
        lax.psum_scatter(
            grad_out_w.astype(jnp.bfloat16), "dp", scatter_dimension=2, tiled=True
        ).astype(jnp.float32),
        lax.psum_scatter(
            grad_key_w.astype(jnp.bfloat16), "dp", scatter_dimension=0, tiled=True
        ).astype(jnp.float32),
        lax.psum_scatter(
            grad_value_w.astype(jnp.bfloat16), "dp", scatter_dimension=0, tiled=True
        ).astype(jnp.float32),
    )
    grad_query_w, grad_out_w, grad_key_w, grad_value_w, grad_in_w, grad_back_w = (
        lax.psum_scatter(
            grad_query_w.astype(jnp.bfloat16), "blk", scatter_dimension=2, tiled=True
        ).astype(jnp.float32),
        lax.psum_scatter(
            grad_out_w.astype(jnp.bfloat16), "blk", scatter_dimension=1, tiled=True
        ).astype(jnp.float32),
        lax.psum_scatter(
            grad_key_w.astype(jnp.bfloat16), "blk", scatter_dimension=1, tiled=True
        ).astype(jnp.float32),
        lax.psum_scatter(
            grad_value_w.astype(jnp.bfloat16), "blk", scatter_dimension=1, tiled=True
        ).astype(jnp.float32),
        lax.psum_scatter(
            grad_in_w.astype(jnp.bfloat16), "blk", scatter_dimension=1, tiled=True
        ).astype(jnp.float32),
        lax.psum_scatter(
            grad_back_w.astype(jnp.bfloat16), "blk", scatter_dimension=1, tiled=True
        ).astype(jnp.float32),
    )
    return (
        result,
        grad_start.astype(jnp.bfloat16),
        grad_gain_one,
        grad_gain_two,
        grad_query_w,
        grad_key_w,
        grad_value_w,
        grad_out_w,
        grad_router_one,
        grad_router_two,
        grad_in_w,
        grad_back_w,
        grad_halt,
    )


def solution(mesh):
    return jax.shard_map(
        on_device,
        mesh=mesh,
        in_specs=(
            P("dp", "blk", None),
            P("dp", None),
            P(None, "dp", "blk", None),
            P(None, "dp", "blk", None),
            P(),
            P(),
            P(None, "dp", "blk"),
            P("dp", "blk"),
            P("dp", "blk"),
            P(None, "blk", "dp"),
            P(),
            P(),
            P("dp", "blk", None),
            P("dp", "blk", None),
            P(),
            P("dp", "blk", None),
        ),
        out_specs=(
            P("dp", "blk", None),
            P("dp", "blk", None),
            P(),
            P(),
            P(None, "dp", "blk"),
            P("dp", "blk"),
            P("dp", "blk"),
            P(None, "blk", "dp"),
            P(),
            P(),
            P("dp", "blk", None),
            P("dp", "blk", None),
            P(),
        ),
        check_vma=False,
    )
```

profile of v0, /device:TPU:0, one launch (start us, length us, event | category | flops | bytes accessed | tf_op | source)
XLA Modules:
  0.0 1174.6 jit_solution(2860506099502796778)
XLA Ops:
  34.4 33.6 %all_gather.33 = bf16[512,512]{1,0:T(8,128)(2,1)S(1)} all-gather(bf16[64,512]{1,0:T(8,128)(2,1)S(1)} %all_gather.32), channel_id=1, replica_groups=mesh['blk'=4,'dp'=8] {'dp'}, dimensions={0}, use_global_device_ids=true | all-gather | bytes 589824 | tf_op jit(solution)/shard_map/all_gather | solution.py:97
  77.7 32.3 %all_gather.31 = bf16[512,512]{1,0:T(8,128)(2,1)S(1)} all-gather(bf16[64,512]{1,0:T(8,128)(2,1)S(1)} %all_gather.30), channel_id=1, replica_groups=mesh['blk'=4,'dp'=8] {'dp'}, dimensions={0}, use_global_device_ids=true | all-gather | bytes 589824 | tf_op jit(solution)/shard_map/all_gather | solution.py:98
  148.0 25.7 %all-gather.7.cloned.1.call-done = bf16[8,512,512]{1,2,0:T(8,128)(2,1)} async-done(((bf16[8,512,64]{1,2,0:T(8,128)(2,1)}), bf16[8,512,512]{1,2,0:T(8,128)(2,1)}) %all-gather.7.cloned.1.call-update) | async-done | bytes 4194320 | tf_op jit(solution)/shard_map/all_gather | solution.py:96
  186.5 21.6 %all-gather.9.cloned.1.call-done = bf16[2,512,2048]{2,1,0:T(8,128)(2,1)} async-done(((bf16[2,128,2048]{2,1,0:T(8,128)(2,1)}), bf16[2,512,2048]{2,1,0:T(8,128)(2,1)}) %all-gather.9.cloned.1.call-update) | async-done | bytes 4194320 | tf_op jit(solution)/shard_map/all_gather | solution.py:91
  208.1 17.4 %fusion.4 = (bf16[8,2,48,2048]{3,2,0,1:T(8,128)(2,1)}, f32[2,8,48,2048]{3,2,1,0:T(8,128)}) fusion(bf16[2,512,2048]{2,1,0:T(8,128)(2,1)} %all-gather.9.cloned.1.call-done, bf16[8,2,48,512]{3,2,1,0:T(8,128)(2,1)S(1)} %all-to-all-done), kind=kOutput, calls=%fused_computation.20 | convolution fusion | flops 1712848896 | bytes 14417920 | tf_op jit(solution)/shard_map/sxcd,xdf->sxcf/dot_general | solution.py:204
  225.5 18.5 %all-gather.11.cloned.1.call-done = bf16[2,2048,512]{2,1,0:T(8,128)(2,1)} async-done(((bf16[2,512,512]{2,1,0:T(8,128)(2,1)}), bf16[2,2048,512]{2,1,0:T(8,128)(2,1)}) %all-gather.11.cloned.1.call-update) | async-done | bytes 4194320 | tf_op jit(solution)/shard_map/all_gather | solution.py:92
  256.6 19.9 %all-to-all-done.1 = bf16[8,2,48,512]{3,2,1,0:T(8,128)(2,1)S(1)} async-done(((bf16[8,2,48,512]{3,2,1,0:T(8,128)(2,1)}), bf16[8,2,48,512]{3,2,1,0:T(8,128)(2,1)S(1)}, u32[]{:S(2)}, u32[]{:S(2)}) %all-to-all-start.1) | async-done | bytes 786464 | tf_op jit(solution)/shard_map/all_to_all | solution.py:209
  339.1 23.3 %all_to_all.40 = bf16[8,2,48,512]{3,2,1,0:T(8,128)(2,1)S(1)} all-to-all(bf16[8,2,48,512]{3,2,1,0:T(8,128)(2,1)S(1)} %bitcast.1069), channel_id=1, replica_groups=mesh['blk'=4,'dp'=8] {'dp'}, dimensions={0} | all-to-all | bytes 1572864 | tf_op jit(solution)/shard_map/all_to_all | solution.py:203
  362.4 17.2 %fusion.7 = (bf16[8,2,48,2048]{3,2,0,1:T(8,128)(2,1)S(1)}, f32[2,8,48,2048]{3,2,1,0:T(8,128)}) fusion(bf16[2,512,2048]{2,1,0:T(8,128)(2,1)} %all-gather.9.cloned.1.call-done, bf16[8,2,48,512]{3,2,1,0:T(8,128)(2,1)S(1)} %all_to_all.40), kind=kOutput, calls=%fused_computation.23 | convolution fusion | flops 1712848896 | bytes 14417920 | tf_op jit(solution)/shard_map/sxcd,xdf->sxcf/dot_general | solution.py:204
  394.2 11.7 all-to-all-done.3
  416.5 23.6 %all_to_all.41 = bf16[8,2,48,512]{3,2,1,0:T(8,128)(2,1)S(1)} all-to-all(bf16[8,2,48,512]{3,2,1,0:T(8,128)(2,1)S(1)} %bitcast.1068), channel_id=1, replica_groups=mesh['blk'=4,'dp'=8] {'dp'}, dimensions={0} | all-to-all | bytes 1572864 | tf_op jit(solution)/shard_map/all_to_all | solution.py:251
  564.1 18.7 %all-to-all-done.6 = bf16[8,2,48,512]{3,2,1,0:T(8,128)(2,1)} async-done(((bf16[8,2,48,512]{3,2,1,0:T(8,128)(2,1)}), bf16[8,2,48,512]{3,2,1,0:T(8,128)(2,1)}, u32[]{:S(2)}, u32[]{:S(2)}) %all-to-all-start.6) | async-done | bytes 786464 | tf_op jit(solution)/shard_map/all_to_all | solution.py:251
  603.5 13.0 %all-to-all-done.7 = bf16[8,2,48,512]{3,2,1,0:T(8,128)(2,1)S(1)} async-done(((bf16[8,2,48,512]{3,2,1,0:T(8,128)(2,1)}), bf16[8,2,48,512]{3,2,1,0:T(8,128)(2,1)S(1)}, u32[]{:S(2)}, u32[]{:S(2)}) %all-to-all-start.7) | async-done | bytes 786464 | tf_op jit(solution)/shard_map/all_to_all | solution.py:265
  715.1 12.8 %reduce-scatter.23.cloned.1.call-done = bf16[64,512]{1,0:T(8,128)(2,1)} async-done(((bf16[512,512]{1,0:T(8,128)(2,1)}), bf16[64,512]{1,0:T(8,128)(2,1)}) %reduce-scatter.23.cloned.1.call-update) | async-done | bytes 65552 | tf_op jit(solution)/shard_map/reduce_scatter | solution.py:450
  737.5 55.0 %reduce-scatter.21.cloned.1.call-done = bf16[64,512]{1,0:T(8,128)(2,1)} async-done(((bf16[512,512]{1,0:T(8,128)(2,1)}), bf16[64,512]{1,0:T(8,128)(2,1)}) %reduce-scatter.21.cloned.1.call-update) | async-done | bytes 65552 | tf_op jit(solution)/shard_map/reduce_scatter | solution.py:447
  817.6 65.5 %reduce-scatter.25.cloned.1.call-done = bf16[8,512,64]{1,2,0:T(8,128)(2,1)} async-done(((bf16[8,512,512]{1,2,0:T(8,128)(2,1)}), bf16[8,512,64]{1,2,0:T(8,128)(2,1)}) %reduce-scatter.25.cloned.1.call-update) | async-done | bytes 524304 | tf_op jit(solution)/shard_map/reduce_scatter | solution.py:444
  897.1 78.0 %reduce-scatter.19.cloned.1.call-done = bf16[8,64,512]{2,0,1:T(8,128)(2,1)} async-done(((bf16[8,512,512]{2,0,1:T(8,128)(2,1)}), bf16[8,64,512]{2,0,1:T(8,128)(2,1)}) %reduce-scatter.19.cloned.1.call-update) | async-done | bytes 524304 | tf_op jit(solution)/shard_map/reduce_scatter | solution.py:441
  975.1 12.5 %copy.597 = bf16[8,64,512]{0,1,2:T(8,128)(2,1)} copy(bf16[8,64,512]{2,0,1:T(8,128)(2,1)} %reduce-scatter.19.cloned.1.call-done) | data formatting | bytes 1048576
  987.7 13.7 %reshape.2278 = bf16[512,512]{1,0:T(8,128)(2,1)} reshape(bf16[512,64,8]{2,1,0:T(8,128)(2,1)} %bitcast.1020) | data formatting | bytes 1048576
  1005.1 42.0 %all-reduce.4 = (f32[512]{0:T(512)}, f32[512]{0:T(512)}, f32[512,8]{0,1:T(8,128)}, f32[512,16]{0,1:T(8,128)}, f32[512]{0:T(512)}) all-reduce(f32[512]{0:T(512)S(1)} %add.437, f32[512]{0:T(512)S(1)} %add.440, f32[512,8]{0,1:T(8,128)S(1)} %convolution_add_fusion.11, ...), channel_id=1, replica_groups=mesh['blk'=4,'dp'=8] {'blk','dp'}, use_global_device_ids=true, to_apply=%region_61.62 | all-reduce | flops 13824 | bytes 110592 | tf_op jit(solution)/shard_map/psum | solution.py:437
  1050.9 15.5 %reduce-scatter.29.cloned.1.call-done = bf16[2,512,512]{2,1,0:T(8,128)(2,1)} async-done(((bf16[2,2048,512]{2,1,0:T(8,128)(2,1)}), bf16[2,512,512]{2,1,0:T(8,128)(2,1)}) %reduce-scatter.29.cloned.1.call-update) | async-done | bytes 1048592 | tf_op jit(solution)/shard_map/reduce_scatter | solution.py:470
  1069.3 44.0 %reduce-scatter.27.cloned.1.call-done = bf16[2,128,2048]{2,1,0:T(8,128)(2,1)} async-done(((bf16[2,512,2048]{2,1,0:T(8,128)(2,1)}), bf16[2,128,2048]{2,1,0:T(8,128)(2,1)}) %reduce-scatter.27.cloned.1.call-update) | async-done | bytes 1048592 | tf_op jit(solution)/shard_map/reduce_scatter | solution.py:467
  1116.1 21.4 %reduce-scatter.37.cloned.1.call-done = bf16[128,512]{1,0:T(8,128)(2,1)} async-done(((bf16[512,512]{1,0:T(8,128)(2,1)}), bf16[128,512]{1,0:T(8,128)(2,1)}) %reduce-scatter.37.cloned.1.call-update) | async-done | bytes 131088
  1139.6 22.2 %reduce-scatter.31.cloned.1.call-done = bf16[128,512]{1,0:T(8,128)(2,1)} async-done(((bf16[512,512]{1,0:T(8,128)(2,1)}), bf16[128,512]{1,0:T(8,128)(2,1)}) %reduce-scatter.31.cloned.1.call-update) | async-done | bytes 131088
  (776 shorter events, 497.9 us)
Async XLA Ops:
  7.3 114.5 %all-gather.5.cloned.1.call-start = ((), (), s32[]{:S(2)}) async-start(), calls=%async_computation.18 | async-start | bytes 4718592 | tf_op jit(solution)/shard_map/all_gather | solution.py:95
  17.7 156.0 %all-gather.7.cloned.1.call-start = ((), (), s32[]{:S(2)}) async-start(), calls=%async_computation.19 | async-start | bytes 4718592 | tf_op jit(solution)/shard_map/all_gather | solution.py:96
  25.8 182.3 %all-gather.9.cloned.1.call-start = ((), (), s32[]{:S(2)}) async-start(), calls=%async_computation.20 | async-start | bytes 5242880 | tf_op jit(solution)/shard_map/all_gather | solution.py:91
  26.5 217.5 %all-gather.11.cloned.1.call-start = ((), (), s32[]{:S(2)}) async-start(), calls=%async_computation.21 | async-start | bytes 5242880 | tf_op jit(solution)/shard_map/all_gather | solution.py:92
  69.5 51.9 %collective-permute-start.1 = (bf16[1,256,512]{2,1,0:T(8,128)(2,1)S(1)}, bf16[1,256,512]{2,1,0:T(8,128)(2,1)S(1)}, u32[]{:S(2)}, u32[]{:S(2)}) collective-permute-start(bf16[1,256,512]{2,1,0:T(8,128)(2,1)S(1)} %bitcast.1089), channel_id=1, source_target_pairs={{0,8},{8,16},{16,24},{1,9},{9,17},{17,25},{2,10},{10,18},{18,26},{... | collective-permute-start | bytes 786440 | tf_op jit(solution)/shard_map/ppermute | solution.py:19
  182.9 25.2 %all-to-all-start = ((bf16[8,2,48,512]{3,2,1,0:T(8,128)(2,1)}), bf16[8,2,48,512]{3,2,1,0:T(8,128)(2,1)S(1)}, u32[]{:S(2)}, u32[]{:S(2)}) async-start(bf16[8,2,48,512]{3,2,1,0:T(8,128)(2,1)} %bitcast.55), calls=%async_computation | async-start | bytes 1572864 | tf_op jit(solution)/shard_map/all_to_all | solution.py:203
  249.9 26.6 %all-to-all-start.1 = ((bf16[8,2,48,512]{3,2,1,0:T(8,128)(2,1)}), bf16[8,2,48,512]{3,2,1,0:T(8,128)(2,1)S(1)}, u32[]{:S(2)}, u32[]{:S(2)}) async-start(bf16[8,2,48,512]{3,2,1,0:T(8,128)(2,1)} %copy.478), calls=%async_computation.1 | async-start | bytes 1572864 | tf_op jit(solution)/shard_map/all_to_all | solution.py:209
  300.9 12.8 %collective-permute-start.2 = (bf16[1,256,512]{2,1,0:T(8,128)(2,1)}, bf16[1,256,512]{2,1,0:T(8,128)(2,1)}, u32[]{:S(2)}, u32[]{:S(2)}) collective-permute-start(bf16[1,256,512]{2,1,0:T(8,128)(2,1)} %bitcast.67), channel_id=1, source_target_pairs={{0,8},{8,16},{16,24},{1,9},{9,17},{17,25},{2,10},{10,18},{18,26},{... | collective-permute-start | bytes 786440 | tf_op jit(solution)/shard_map/ppermute | solution.py:19
  382.3 23.5 %all-to-all-start.3 = ((bf16[8,2,48,512]{3,2,1,0:T(8,128)(2,1)}), bf16[8,2,48,512]{3,2,1,0:T(8,128)(2,1)S(1)}, u32[]{:S(2)}, u32[]{:S(2)}) async-start(bf16[8,2,48,512]{3,2,1,0:T(8,128)(2,1)} %copy.500), calls=%async_computation.3 | async-start | bytes 1572864 | tf_op jit(solution)/shard_map/all_to_all | solution.py:209
  449.0 23.9 %all-to-all-start.5 = ((bf16[8,2,48,512]{3,2,1,0:T(8,128)(2,1)}), bf16[8,2,48,512]{3,2,1,0:T(8,128)(2,1)S(1)}, u32[]{:S(2)}, u32[]{:S(2)}) async-start(bf16[8,2,48,512]{3,2,1,0:T(8,128)(2,1)} %copy.503), calls=%async_computation.5 | async-start | bytes 1572864 | tf_op jit(solution)/shard_map/all_to_all | solution.py:265
  521.2 25.2 %collective-permute-start.5 = (bf16[1,256,512]{1,2,0:T(8,128)(2,1)}, bf16[1,256,512]{1,2,0:T(8,128)(2,1)}, u32[]{:S(2)}, u32[]{:S(2)}) collective-permute-start(bf16[1,256,512]{1,2,0:T(8,128)(2,1)} %slice.522), channel_id=1, source_target_pairs={{8,0},{16,8},{24,16},{9,1},{17,9},{25,17},{10,2},{18,10},{26,18},{... | collective-permute-start | bytes 786440 | tf_op jit(solution)/shard_map/ppermute | solution.py:19
  527.9 18.1 %collective-permute-start.4 = (bf16[1,256,512]{1,2,0:T(8,128)(2,1)}, bf16[1,256,512]{1,2,0:T(8,128)(2,1)S(1)}, u32[]{:S(2)}, u32[]{:S(2)}) collective-permute-start(bf16[1,256,512]{1,2,0:T(8,128)(2,1)} %slice.523), channel_id=1, source_target_pairs={{8,0},{16,8},{24,16},{9,1},{17,9},{25,17},{10,2},{18,10},{26,18},{... | collective-permute-start | bytes 786440 | tf_op jit(solution)/shard_map/ppermute | solution.py:19
  557.8 25.1 %all-to-all-start.6 = ((bf16[8,2,48,512]{3,2,1,0:T(8,128)(2,1)}), bf16[8,2,48,512]{3,2,1,0:T(8,128)(2,1)}, u32[]{:S(2)}, u32[]{:S(2)}) async-start(bf16[8,2,48,512]{3,2,1,0:T(8,128)(2,1)} %bitcast.1067), calls=%async_computation.6 | async-start | bytes 1572864 | tf_op jit(solution)/shard_map/all_to_all | solution.py:251
  591.9 24.6 %all-to-all-start.7 = ((bf16[8,2,48,512]{3,2,1,0:T(8,128)(2,1)}), bf16[8,2,48,512]{3,2,1,0:T(8,128)(2,1)S(1)}, u32[]{:S(2)}, u32[]{:S(2)}) async-start(bf16[8,2,48,512]{3,2,1,0:T(8,128)(2,1)} %copy.525), calls=%async_computation.7 | async-start | bytes 1572864 | tf_op jit(solution)/shard_map/all_to_all | solution.py:265
  596.1 131.8 %reduce-scatter.23.cloned.1.call-start = ((), (), s32[]{:S(2)}) async-start(), calls=%async_computation.24 | async-start | bytes 589824 | tf_op jit(solution)/shard_map/reduce_scatter | solution.py:450
  666.1 126.3 %reduce-scatter.21.cloned.1.call-start = ((), (), s32[]{:S(2)}) async-start(), calls=%async_computation.23 | async-start | bytes 589824 | tf_op jit(solution)/shard_map/reduce_scatter | solution.py:447
  675.8 207.3 %reduce-scatter.25.cloned.1.call-start = ((), (), s32[]{:S(2)}) async-start(), calls=%async_computation.25 | async-start | bytes 4718592 | tf_op jit(solution)/shard_map/reduce_scatter | solution.py:444
  683.7 291.4 %reduce-scatter.19.cloned.1.call-start = ((), (), s32[]{:S(2)}) async-start(), calls=%async_computation.22 | async-start | bytes 4718592 | tf_op jit(solution)/shard_map/reduce_scatter | solution.py:441
  715.0 333.0 %reduce-scatter.35.cloned.1.call-start = ((), (), s32[]{:S(2)}) async-start(), calls=%async_computation.30 | async-start | bytes 163840
  729.5 319.9 %reduce-scatter.33.cloned.1.call-start = ((), (), s32[]{:S(2)}) async-start(), calls=%async_computation.29 | async-start | bytes 163840
  794.1 272.4 %reduce-scatter.29.cloned.1.call-start = ((), (), s32[]{:S(2)}) async-start(), calls=%async_computation.27 | async-start | bytes 5242880 | tf_op jit(solution)/shard_map/reduce_scatter | solution.py:470
  803.0 310.3 %reduce-scatter.27.cloned.1.call-start = ((), (), s32[]{:S(2)}) async-start(), calls=%async_computation.26 | async-start | bytes 5242880 | tf_op jit(solution)/shard_map/reduce_scatter | solution.py:467
  812.3 325.3 %reduce-scatter.37.cloned.1.call-start = ((), (), s32[]{:S(2)}) async-start(), calls=%async_computation.31 | async-start | bytes 655360
  888.4 273.3 %reduce-scatter.31.cloned.1.call-start = ((), (), s32[]{:S(2)}) async-start(), calls=%async_computation.28 | async-start | bytes 655360
  (217 other events, 4298.5 us)
Sparse Core Ops, SparseCore 0:
  17.8 81.3 all-gather.4
  101.4 72.2 all-gather.6
  175.3 32.7 all-gather.8
  209.5 34.4 all-gather.10
  666.2 61.6 reduce-scatter.22
  731.5 60.9 reduce-scatter.20
  796.1 87.0 reduce-scatter.24
  887.2 87.8 reduce-scatter.18
  977.5 19.3 reduce-scatter.34
  999.3 19.5 reduce-scatter.32
  1021.4 44.9 reduce-scatter.28
  1069.0 44.2 reduce-scatter.26
  1115.8 21.6 reduce-scatter.36
  1140.0 21.6 reduce-scatter.30
where the time goes:
time: 1180 us; the launch traced here: 1170 us
  waiting for transfers between devices  452 us (38%)
  matrix products  255 us (22%)
  blocking collectives  186 us (16%)
  local copies, waits for them, and re-layouts  149 us (13%)
  other arithmetic  75 us (6%)
  starting transfers between devices  40.1 us (3%)
  between operations  17.5 us (1%)
    reduce_scatter x1, waiting for transfers between devices, on_device(): lax.psum_scatter(grad_query_w.astype(jnp.bfloat16), 'dp', scatter_dimensi...  78 us
    reduce_scatter x1, waiting for transfers between devices, on_device(): lax.psum_scatter(grad_out_w.astype(jnp.bfloat16), 'dp', scatter_dimension...  65.5 us
    reduce_scatter x1, waiting for transfers between devices, on_device(): lax.psum_scatter(grad_key_w.astype(jnp.bfloat16), 'dp', scatter_dimension...  55 us
    unnamed x440, local copies, waits for them, and re-layouts  50.9 us
    unnamed x18, waiting for transfers between devices  44.5 us
    reduce_scatter x1, waiting for transfers between devices, on_device(): lax.psum_scatter(grad_in_w.astype(jnp.bfloat16), 'blk', scatter_dimension...  44 us
    psum x1, blocking collectives, on_device(): lax.psum((grad_gain_one, grad_gain_two, grad_router_one, grad_router_two,...  42 us
    dot_general x2, matrix products, step_forward(): jnp.einsum('sxcd,xdf->sxcf', arrived, local_in, preferred_element_type=jn...  34.6 us
  transfers between devices with their start and end apart: 28, of which 17 were waited for; matrix products, arithmetic and copies ran while one was open for 23% of the time, Pallas kernels for 0%

commit v1 on v0

v1 whole, which is shorter than its diff:
```python
import functools
from typing import NamedTuple

import jax
import jax.numpy as jnp
from jax import lax
from jax.experimental import pallas as pl
from jax.experimental.pallas import tpu as pltpu
from jax.sharding import PartitionSpec as P

HEADS = 8
HD = 64
MAXLEN = 256
QROWS = 128
WINDOW = MAXLEN + QROWS
LANES = 128
EPSILON = 1e-06
MASKED_SCORE = -1e30
MESH = pl.DeviceIdType.MESH
BF = jnp.bfloat16
F32 = jnp.float32
VMEM_BYTES = 58 * 2**20


class Plan(NamedTuple):
    blk: int
    dp: int
    lo: int
    hi: int
    seq: int
    width: int
    heads: int
    mixers: int
    top: int
    experts: int
    local: int
    group: int
    cap: int
    ff: int

    @property
    def length(self):
        return self.blk * self.seq

    @property
    def cols(self):
        return self.heads * HD

    @property
    def qkv(self):
        return (self.mixers + 2) * self.cols

    @property
    def all_cols(self):
        return (2 * self.mixers + 2) * self.cols

    @property
    def blocks(self):
        return self.length // QROWS

    @property
    def slots(self):
        return self.experts * self.cap

    @property
    def chips(self):
        return self.blk // 2


def mm(a, b):
    return lax.dot_general(a, b, (((1,), (0,)), ((), ())), preferred_element_type=F32)


def mm_nt(a, b):
    return lax.dot_general(a, b, (((1,), (1,)), ((), ())), preferred_element_type=F32)


def place():
    return lax.axis_index("blk"), lax.axis_index("dp")


def turn(index, by, size):
    return lax.rem(index + (by % size), size)


def greet(peers):
    barrier = pltpu.get_barrier_semaphore()
    for peer in peers:
        pl.semaphore_signal(barrier, inc=1, device_id=peer, device_id_type=MESH)
    pl.semaphore_wait(barrier, len(peers))


def send(src, dst, sems, slot, peer):
    copy = pltpu.make_async_remote_copy(
        src_ref=src,
        dst_ref=dst,
        send_sem=sems[0].at[slot],
        recv_sem=sems[1].at[slot],
        device_id=peer,
        device_id_type=MESH,
    )
    copy.start()
    return copy


def aligned(value, by):
    return pl.multiple_of(value, by)


def pack_peers(p):
    b, d = place()
    y, c = b // 2, lax.rem(b, 2)
    peers = [(2 * y + 1 - c, d)]
    return peers + [(2 * turn(y, s, p.chips) + c, d) for s in range(1, p.chips)]


def slot_peer(p, s):
    b, d = place()
    e, g = b // p.group, lax.rem(b, p.group)
    return (turn(e, s // p.dp, p.local) * p.group + g, turn(d, s % p.dp, p.dp))


def slot_peers(p):
    return [slot_peer(p, s) for s in range(1, p.experts)]


def slot_source(p, s):
    b, d = place()
    e, g = b // p.group, lax.rem(b, p.group)
    return (turn(e, -(s // p.dp), p.local) * p.group + g, turn(d, -(s % p.dp), p.dp))


def dp_peers(p):
    b, d = place()
    z, x = d // p.lo, lax.rem(d, p.lo)
    peers = [(b, turn(z, s, p.hi) * p.lo + x) for s in range(1, p.hi)]
    return peers + [(b, z * p.lo + turn(x, t, p.lo)) for t in range(1, p.lo)]


def expert_peers(p):
    b, d = place()
    e, g = b // p.group, lax.rem(b, p.group)
    peers = [(turn(e, s, p.local) * p.group + g, d) for s in range(1, p.local)]
    return peers + [(e * p.group + turn(g, t, p.group), d) for t in range(1, p.group)]


class PackGather:
    def __init__(self, p, buf, far, near):
        self.p, self.buf, self.far, self.near = p, buf, far, near

    def begin(self):
        p = self.p
        b, d = place()
        y, c = b // 2, lax.rem(b, 2)
        own = self.buf.at[b]
        self.first = [
            send(own, own, self.far, s - 1, (2 * turn(y, s, p.chips) + c, d))
            for s in range(1, p.chips)
        ]
        self.second = [send(own, own, self.near, 0, (2 * y + 1 - c, d))]

    def finish(self):
        p = self.p
        b, d = place()
        y, c = b // 2, lax.rem(b, 2)
        for s in range(1, p.chips):
            self.first[s - 1].wait_recv()
            block = self.buf.at[2 * turn(y, -s, p.chips) + c]
            self.second.append(send(block, block, self.near, s, (2 * y + 1 - c, d)))
        for copy in self.second:
            copy.wait()
        for copy in self.first:
            copy.wait_send()


def pack_sems(p):
    return [
        pltpu.SemaphoreType.DMA((max(1, p.chips - 1),)),
        pltpu.SemaphoreType.DMA((max(1, p.chips - 1),)),
        pltpu.SemaphoreType.DMA((p.chips,)),
        pltpu.SemaphoreType.DMA((p.chips,)),
    ]


def pack_sum(p, make, part, own, near_in, far_out, far_in, sems):
    near, far = (sems[2], sems[3]), (sems[0], sems[1])
    b, d = place()
    y, c = b // 2, lax.rem(b, 2)
    order = [turn(y, s, p.chips) for s in list(range(1, p.chips)) + [0]]
    first = []
    for k, yy in enumerate(order):
        other = 2 * yy + 1 - c
        part[other] = make(other).astype(BF)
        first.append(send(part.at[other], near_in.at[k], near, k, (2 * y + 1 - c, d)))
    second = []
    for k, yy in enumerate(order):
        term = make(2 * yy + c)
        first[k].wait_recv()
        term = term + near_in[k].astype(F32)
        if k < p.chips - 1:
            far_out[k] = term.astype(BF)
            second.append(send(far_out.at[k], far_in.at[k], far, k, (2 * yy + c, d)))
        else:
            own[...] = term
    total = own[...]
    for k, copy in enumerate(second):
        copy.wait_recv()
        total = total + far_in[k].astype(F32)
    for copy in first + second:
        copy.wait_send()
    return total


def slot_send(p, src, dst, sems, s, peer):
    rows = pl.ds(s * p.cap, p.cap)
    return send(src.at[rows], dst.at[rows], sems, s, peer)


def setup_kernel(p, wall, win, wback, picks, routes, all_w, all_in, all_back, all_picks, disp, comb, both, mine, *sems):
    b, d = place()
    z, x = d // p.lo, lax.rem(d, p.lo)
    e, g = b // p.group, lax.rem(b, p.group)
    hi, lo, wide, near, pack, slot = (sems[2 * k : 2 * k + 2] for k in range(6))
    pack = sems[8:12]
    slot = sems[12:14]
    local = sems[14]
    greet(pack_peers(p) + slot_peers(p) + dp_peers(p) + expert_peers(p))
    own_rows = wall.shape[0]
    in_rows, back_rows = win.shape[1], wback.shape[1]

    def dp_rows(index):
        return all_w.at[pl.ds(aligned(index * own_rows, own_rows), own_rows)]

    def in_at(index):
        return all_in.at[pl.ds(aligned(index * in_rows, in_rows), in_rows)]

    def back_at(index):
        return all_back.at[pl.ds(aligned(index * back_rows, back_rows), back_rows)]

    waits = []
    here = [
        pltpu.make_async_copy(wall, dp_rows(d), local.at[0]),
        pltpu.make_async_copy(win.at[e], in_at(b), local.at[1]),
        pltpu.make_async_copy(wback.at[e], back_at(b), local.at[2]),
    ]
    for copy in here:
        copy.start()
    along = [send(wall, dp_rows(d), hi, s - 1, (b, turn(z, s, p.hi) * p.lo + x)) for s in range(1, p.hi)]
    for t in range(1, p.lo):
        waits.append(send(wall, dp_rows(d), lo, t - 1, (b, z * p.lo + turn(x, t, p.lo))))
    over = []
    for s in range(1, p.local):
        to = turn(e, s, p.local)
        over.append(send(win.at[to], in_at(b), wide, 2 * s - 2, (to * p.group + g, d)))
        over.append(send(wback.at[to], back_at(b), wide, 2 * s - 1, (to * p.group + g, d)))
    for t in range(1, p.group):
        to = e * p.group + turn(g, t, p.group)
        waits.append(send(win.at[e], in_at(b), near, 2 * t - 2, (to, d)))
        waits.append(send(wback.at[e], back_at(b), near, 2 * t - 1, (to, d)))

    all_picks[b] = picks[...]
    spread = PackGather(p, all_picks, pack[0:2], pack[2:4])
    spread.begin()

    place_in = lax.broadcasted_iota(jnp.int32, (p.experts, 1), 0)
    ids = lax.rem(d + lax.rem(place_in, p.dp), p.dp) * p.local + lax.rem(e + place_in // p.dp, p.local)
    earlier = (
        lax.broadcasted_iota(jnp.int32, (p.seq, p.seq), 0) < lax.broadcasted_iota(jnp.int32, (p.seq, p.seq), 1)
    ).astype(BF)
    slot_ids = lax.broadcasted_iota(jnp.int32, (p.cap, p.seq), 0).astype(F32)
    lane_ids = lax.broadcasted_iota(jnp.int32, (LANES, 1), 0)
    sent = []
    for step in range(2):
        one, two = routes[2 * step : 2 * step + 1, :], routes[2 * step + 1 : 2 * step + 2, :]
        member = jnp.where((one == ids) | (two == ids), 1.0, 0.0)
        rank = mm(member.astype(BF), earlier)
        rank = jnp.where(member > 0.5, rank, -1.0)
        for s in range(p.experts):
            disp[step, pl.ds(s * p.cap, p.cap), :] = jnp.where(rank[s : s + 1, :] == slot_ids, 1.0, 0.0).astype(BF)
        table = disp[step]
        comb[step] = table.astype(F32).T.astype(BF)
        pair = jnp.where((one == lane_ids) | (two == lane_ids), 1.0, 0.0).astype(BF)
        both[step] = mm_nt(table, pair).astype(BF)
        mine[step, 0 : p.cap, :] = both[step, 0 : p.cap, :]
        for s in range(1, p.experts):
            rows = pl.ds(s * p.cap, p.cap)
            sent.append(
                send(both.at[step, rows], mine.at[step, rows], slot, step * p.experts + s, slot_peer(p, s))
            )

    for s in range(1, p.hi):
        along[s - 1].wait_recv()
        rows = dp_rows(turn(z, -s, p.hi) * p.lo + x)
        for t in range(1, p.lo):
            k = s * (p.lo - 1) + t - 1
            waits.append(send(rows, rows, lo, k, (b, z * p.lo + turn(x, t, p.lo))))
    spread.finish()
    for s in range(1, p.local):
        source = turn(e, -s, p.local) * p.group + g
        for which, rows in ((0, in_at(source)), (1, back_at(source))):
            over[2 * s - 2 + which].wait_recv()
            for t in range(1, p.group):
                k = (s * (p.group - 1) + t - 1) * 2 + which
                waits.append(send(rows, rows, near, k, (e * p.group + turn(g, t, p.group), d)))
    for copy in waits + sent:
        copy.wait()
    for copy in along + over:
        copy.wait_send()
    for copy in here:
        copy.wait()


def attention_mask(seg_cols, seg_rows, start):
    keys = seg_cols[pl.ds(start, WINDOW), :]
    queries = seg_rows[:, pl.ds(start, QROWS)]
    key_at = lax.broadcasted_iota(jnp.int32, (WINDOW, QROWS), 0) - MAXLEN
    query_at = lax.broadcasted_iota(jnp.int32, (WINDOW, QROWS), 1)
    return jnp.where((key_at <= query_at) & (keys == queries), 0.0, MASKED_SCORE)


def head_rows(p, dst, values):
    flat = values.T
    lane = lax.broadcasted_iota(jnp.int32, flat.shape, 1) // HD
    for h in range(p.heads):
        dst(h, jnp.where(lane == h, flat, 0.0).astype(BF))


def pick_rows(p, routes, terms):
    picked = []
    for j in range(p.top):
        row = routes[j : j + 1, :]
        total = None
        for e in range(p.mixers):
            term = jnp.where(row == e, terms(e), 0.0)
            total = term if total is None else total + term
        picked.append(total)
    return picked


def spread_rows(p, routes, values, e):
    total = None
    for j in range(p.top):
        term = jnp.where(routes[j : j + 1, :] == e, values[j], 0.0)
        total = term if total is None else total + term
    return total


def attention_forward_kernel(
    p, step, h_ref, gain_one, gain_two, w_ref, router, picks, seg_rows, seg_cols,
    middle, m_ref, nt, qs, kt, vt, lse, att, mix, gates,
    w_t, k_heads, part, own, near_in, far_out, far_in, *sems,
):
    b, _ = place()
    cols, top = p.cols, p.top
    greet(pack_peers(p))
    h = h_ref[...]
    inverse = lax.rsqrt(jnp.mean(h * h, axis=-1, keepdims=True) + EPSILON)
    nt[b] = (h * inverse * gain_one[...]).T.astype(BF)
    spread = PackGather(p, nt, sems[0:2], sems[2:4])
    spread.begin()
    for start in range(0, p.qkv, 2 * cols):
        w_t[start : start + 2 * cols, :] = w_ref[:, start : start + 2 * cols].astype(F32).T.astype(BF)
    k_heads[:, 0:MAXLEN, :] = jnp.zeros((p.heads, MAXLEN, cols), BF)
    kt[:, 0:MAXLEN] = jnp.zeros((cols, MAXLEN), BF)
    vt[:, 0:MAXLEN] = jnp.zeros((cols, MAXLEN), BF)
    spread.finish()

    @pl.loop(0, p.blk)
    def _(bb):
        states = nt[bb]
        table = picks[bb, step * top : (step + 1) * top, :]
        logits = mm(router[...], states)
        chosen = pick_rows(p, table, lambda e: logits[e : e + 1, :])
        peak = functools.reduce(jnp.maximum, chosen)
        chosen = [jnp.exp(row - peak) for row in chosen]
        scale = 1.0 / sum(chosen)
        for j in range(top):
            gates[bb, j : j + 1, :] = chosen[j] * scale
        values = mm(w_t[...], states)
        for k in range(p.seq // QROWS):
            lanes = slice(k * QROWS, (k + 1) * QROWS)
            queries = pick_rows(
                p, table[:, lanes], lambda e: values[e * cols : (e + 1) * cols, lanes]
            )
            for j in range(top):
                qs[bb * (p.seq // QROWS) + k, :, j * QROWS : (j + 1) * QROWS] = (
                    queries[j] * (HD**-0.5)
                ).astype(BF)
        at = aligned(MAXLEN + bb * p.seq, QROWS)
        keys = values[p.mixers * cols : (p.mixers + 1) * cols, :]
        kt[:, pl.ds(at, p.seq)] = keys.astype(BF)
        vt[:, pl.ds(at, p.seq)] = values[(p.mixers + 1) * cols :, :].astype(BF)

        def put(head, rows):
            k_heads[head, pl.ds(at, p.seq), :] = rows

        head_rows(p, put, keys)

    @pl.loop(0, p.blocks)
    def _(i):
        start = aligned(i * QROWS, QROWS)
        bias = attention_mask(seg_cols, seg_rows, start)
        bias = jnp.concatenate([bias] * top, axis=1)
        queries = qs[i]
        for head in range(p.heads):
            scores = mm(k_heads[head, pl.ds(start, WINDOW), :], queries) + bias
            peak = jnp.max(scores, axis=0, keepdims=True)
            scores = jnp.exp(scores - peak)
            total = jnp.sum(scores, axis=0, keepdims=True)
            lse[i, head : head + 1, :] = peak + jnp.log(total)
            probs = (scores * (1.0 / total)).astype(BF)
            rows = slice(head * HD, (head + 1) * HD)
            att[i, rows, :] = mm(vt[rows, pl.ds(start, WINDOW)], probs).astype(BF)
        bb = i // (p.seq // QROWS)
        at = pl.ds(aligned(lax.rem(i, p.seq // QROWS) * QROWS, QROWS), QROWS)
        table = picks[bb, step * top : (step + 1) * top, at]
        weights = gates[bb, 0:top, at]
        values = [
            att[i, :, j * QROWS : (j + 1) * QROWS].astype(F32) * weights[j : j + 1, :] for j in range(top)
        ]
        for e in range(p.mixers):
            mix[e * cols : (e + 1) * cols, pl.ds(start, QROWS)] = spread_rows(p, table, values, e).astype(BF)

    def branch(index):
        lanes = pl.ds(aligned(index * p.seq, p.seq), p.seq)
        return mm(w_ref[:, p.qkv :], mix[:, lanes])

    total = pack_sum(p, branch, part, own, near_in, far_out, far_in, sems[4:8])
    state = h_ref[...] + total.T
    middle[...] = state
    inverse = lax.rsqrt(jnp.mean(state * state, axis=-1, keepdims=True) + EPSILON)
    m_ref[...] = (state * inverse * gain_two[...]).astype(BF)


def attention_backward_kernel(
    p, step, first, grad_ref, base_ref, h_ref, gain_one, w_ref, router_col, picks, seg_rows, seg_cols,
    nt, qs, kt, vt, lse, att, mix, gates, *rest,
):
    if first:
        before, router_before, gain_before = None, None, None
    else:
        before, router_before, gain_before = rest[0:3]
        rest = rest[3:]
    grad_in, grad_w, grad_router, grad_gain = rest[0:4]
    gt, wo, k_heads, v_heads, da, dlog, dkt, dvt, dall, part, own, near_in, far_out, far_in = rest[4:18]
    sems = rest[18:]
    b, _ = place()
    cols, top = p.cols, p.top
    sub = p.seq // QROWS
    greet(pack_peers(p))
    gt[b] = grad_ref[...].T.astype(BF)
    spread = PackGather(p, gt, sems[0:2], sems[2:4])
    spread.begin()
    for start in range(0, p.mixers * cols, 2 * cols):
        piece = w_ref[:, p.qkv + start : p.qkv + start + 2 * cols]
        wo[start : start + 2 * cols, :] = piece.astype(F32).T.astype(BF)
    dkt[...] = jnp.zeros_like(dkt)
    dvt[...] = jnp.zeros_like(dvt)

    @pl.loop(0, (p.length + MAXLEN) // QROWS)
    def _(k):
        at = aligned(k * QROWS, QROWS)

        def put_key(head, rows):
            k_heads[head, pl.ds(at, QROWS), :] = rows

        def put_value(head, rows):
            v_heads[head, pl.ds(at, QROWS), :] = rows

        head_rows(p, put_key, kt[:, pl.ds(at, QROWS)].astype(F32))
        head_rows(p, put_value, vt[:, pl.ds(at, QROWS)].astype(F32))

    spread.finish()

    @pl.loop(0, p.blk)
    def _(bb):
        table = picks[bb, step * top : (step + 1) * top, :]
        weights = gates[bb, 0:top, :]
        values = mm(wo[...], gt[bb])
        for k in range(sub):
            lanes = slice(k * QROWS, (k + 1) * QROWS)
            here = table[:, lanes]
            picked = pick_rows(p, here, lambda e: values[e * cols : (e + 1) * cols, lanes])
            grads = []
            for j in range(top):
                slot = slice(j * QROWS, (j + 1) * QROWS)
                past = att[bb * sub + k, :, slot].astype(F32)
                grads.append(jnp.sum(picked[j] * past, axis=0, keepdims=True))
                da[bb * sub + k, :, slot] = (picked[j] * weights[j : j + 1, lanes]).astype(BF)
            mean = sum(weights[j : j + 1, lanes] * grads[j] for j in range(top))
            back = [weights[j : j + 1, lanes] * (grads[j] - mean) for j in range(top)]
            for e in range(p.mixers):
                dlog[bb, e : e + 1, lanes] = spread_rows(p, here, back, e)

    @pl.loop(0, p.blocks)
    def _(i):
        start = aligned(i * QROWS, QROWS)
        keys = pl.ds(start, WINDOW)
        bias = attention_mask(seg_cols, seg_rows, start)
        bias = jnp.concatenate([bias] * top, axis=1)
        queries = qs[i]
        grads = da[i]
        past = att[i]
        query_grads = []
        for head in range(p.heads):
            rows = slice(head * HD, (head + 1) * HD)
            scores = mm(k_heads[head, keys, :], queries) + bias
            probs = jnp.exp(scores - lse[i, head : head + 1, :])
            mean = jnp.sum(grads[rows].astype(F32) * past[rows].astype(F32), axis=0, keepdims=True)
            dscores = (probs * (mm(v_heads[head, keys, :], grads) - mean)).astype(BF)
            dvt[rows, keys] += mm_nt(grads[rows], probs.astype(BF))
            dkt[rows, keys] += mm_nt(queries[rows], dscores)
            query_grads.append(mm(kt[rows, keys], dscores) * (HD**-0.5))
        bb = i // sub
        at = pl.ds(aligned(lax.rem(i, sub) * QROWS, QROWS), QROWS)
        table = picks[bb, step * top : (step + 1) * top, at]
        merged = jnp.concatenate(query_grads, axis=0)
        values = [merged[:, j * QROWS : (j + 1) * QROWS] for j in range(top)]
        for e in range(p.mixers):
            dall[e * cols : (e + 1) * cols, pl.ds(start, QROWS)] = spread_rows(p, table, values, e).astype(BF)

    dall[p.mixers * cols : (p.mixers + 1) * cols, :] = dkt[:, MAXLEN:].astype(BF)
    dall[(p.mixers + 1) * cols :, :] = dvt[:, MAXLEN:].astype(BF)

    def branch(index):
        lanes = pl.ds(aligned(index * p.seq, p.seq), p.seq)
        return mm(w_ref[:, : p.qkv], dall[:, lanes]) + mm(router_col[...], dlog[index].astype(BF))

    total = pack_sum(p, branch, part, own, near_in, far_out, far_in, sems[4:8])
    grad_n = total.T
    h = h_ref[...]
    inverse = lax.rsqrt(jnp.mean(h * h, axis=-1, keepdims=True) + EPSILON)
    scaled = grad_n * gain_one[...]
    back = inverse * scaled - h * (inverse * inverse * inverse) * jnp.mean(scaled * h, axis=-1, keepdims=True)
    grad_in[...] = (base_ref[...] + grad_ref[...] + back if first else grad_ref[...] + back).astype(grad_in.dtype)
    gain = jnp.sum(grad_n * h * inverse, axis=0, keepdims=True)
    grad_gain[...] = gain if first else gain_before[...] + gain
    router = sum(mm_nt(dlog[bb].astype(BF), nt[bb]) for bb in range(p.blk))
    grad_router[...] = router if first else router_before[...] + router
    tile = 2 * cols
    for start in range(0, p.all_cols, tile):
        total = None
        for bb in range(p.blk):
            lanes = slice(bb * p.seq, (bb + 1) * p.seq)
            if start < p.qkv:
                term = mm_nt(nt[bb], dall[start : start + tile, lanes])
            else:
                term = mm_nt(gt[bb], mix[start - p.qkv : start - p.qkv + tile, lanes])
            total = term if total is None else total + term
        at = slice(start, start + tile)
        grad_w[:, at] = total if first else before[:, at] + total


def own_lane(p):
    b, d = place()
    mine = d * p.local + b // p.group
    return jnp.where(lax.broadcasted_iota(jnp.int32, (1, LANES), 1) == mine, 1.0, 0.0)


def slot_gates(p, rows, pair, router):
    own = own_lane(p)
    logits = mm(rows, router)
    return 1.0 / (1.0 + jnp.exp(jnp.sum(logits * (pair - 2.0 * own), axis=-1, keepdims=True)))


def gelu_of(inner):
    return inner * (0.5 * (1.0 + lax.erf(inner * 0.7071067811865476)))


def gelu_both(inner):
    half = 0.5 * (1.0 + lax.erf(inner * 0.7071067811865476))
    slope = half + inner * jnp.exp(-0.5 * inner * inner) * 0.3989422804014327
    return inner * half, slope


FTILE = 512


def expert_forward(p, rows, w_in, w_back):
    total = None
    for start in range(0, p.ff, FTILE):
        at = slice(start, start + FTILE)
        act = gelu_of(mm(rows, w_in[:, at])).astype(BF)
        term = mm(act, w_back[at, :])
        total = term if total is None else total + term
    return total


def expert_backward(p, arrived, grads, w_in, w_back, grad_w_in, grad_w_back, before_in, before_back, arrived_t, grad_rows):
    arrived_t[...] = arrived[...].astype(F32).T.astype(BF)
    for k, start in enumerate(range(0, p.ff, FTILE)):
        at = slice(start, start + FTILE)
        act, slope = gelu_both(mm(arrived[...], w_in[:, at]))
        act_t = act.T.astype(BF)
        rows = grads[...]
        term = mm(act_t, rows)
        grad_w_back[at, :] = term if before_back is None else before_back[at, :] + term
        inner = (mm_nt(rows, w_back[at, :]) * slope).astype(BF)
        term = mm(arrived_t[...], inner)
        grad_w_in[:, at] = term if before_in is None else before_in[:, at] + term
        term = mm_nt(inner, w_in[:, at])
        if k == 0:
            grad_rows[...] = term
        else:
            grad_rows[...] += term


def router_back(p, gate, dots, pair, arrived, router, grad_rows):
    coeff = gate * (1.0 - gate) * dots * (2.0 * own_lane(p) - pair)
    grad_rows[...] += mm_nt(coeff.astype(BF), router)
    return mm(coeff.T.astype(BF), arrived)


def expert_forward_kernel(
    p, m_ref, middle, disp, comb, pair, w_in, w_back, router,
    out_ref, arrived, produced, outgoing, ret_out, ret_in, *sems,
):
    greet(slot_peers(p))
    outgoing[...] = mm(disp[...], m_ref[...]).astype(BF)
    arrived[0 : p.cap, :] = outgoing[0 : p.cap, :]
    there = {s: slot_send(p, outgoing, arrived, sems[0:2], s, slot_peer(p, s)) for s in range(1, p.experts)}
    back = []
    per = max(1, p.experts // 4)
    for first in range(0, p.experts, per):
        for s in range(max(first, 1), first + per):
            there[s].wait_recv()
        at = pl.ds(first * p.cap, per * p.cap)
        rows = arrived[at, :]
        out = expert_forward(p, rows, w_in, w_back)
        produced[at, :] = out.astype(BF)
        ret_out[at, :] = (out * slot_gates(p, rows, pair[at, :].astype(F32), router[...])).astype(BF)
        for s in range(max(first, 1), first + per):
            back.append(slot_send(p, ret_out, ret_in, sems[2:4], s, slot_source(p, s)))
    ret_in[0 : p.cap, :] = ret_out[0 : p.cap, :]
    for copy in back:
        copy.wait()
    for copy in there.values():
        copy.wait_send()
    out_ref[...] = middle[...] + mm(comb[...], ret_in[...])


def norm_two_back(middle, gain, grad_m, grad_out):
    state = middle[...]
    inverse = lax.rsqrt(jnp.mean(state * state, axis=-1, keepdims=True) + EPSILON)
    scaled = grad_m * gain[...]
    back = inverse * scaled - state * (inverse * inverse * inverse) * jnp.mean(
        scaled * state, axis=-1, keepdims=True
    )
    return grad_out + back, jnp.sum(grad_m * state * inverse, axis=0, keepdims=True)


def expert_both_kernel(
    p, m_ref, middle, first_ref, cot_ref, halt, gain_two, disp, comb, pair, w_in, w_back, router,
    result, grad_first, grad_middle, grad_gain, grad_halt, grad_w_in, grad_w_back, grad_router,
    outgoing, arrived, u_out, u_in, ret_out, ret_in, gret_out, gret_in, arrived_t, grads, grad_rows, produced, *sems,
):
    greet(slot_peers(p))
    outgoing[...] = mm(disp[...], m_ref[...]).astype(BF)
    arrived[0 : p.cap, :] = outgoing[0 : p.cap, :]
    there = {s: slot_send(p, outgoing, arrived, sems[0:2], s, slot_peer(p, s)) for s in range(1, p.experts)}
    first = first_ref[...]
    cot = cot_ref[...].astype(F32)
    stop = 1.0 / (1.0 + jnp.exp(-jnp.sum(first * halt[...], axis=-1, keepdims=True)))
    u_out[...] = mm(disp[...], ((1.0 - stop) * cot).astype(BF)).astype(BF)
    u_in[0 : p.cap, :] = u_out[0 : p.cap, :]
    there_u = [slot_send(p, u_out, u_in, sems[4:6], s, slot_peer(p, s)) for s in range(1, p.experts)]
    back = []
    per = max(1, p.experts // 4)
    for begin in range(0, p.experts, per):
        for s in range(max(begin, 1), begin + per):
            there[s].wait_recv()
        at = pl.ds(begin * p.cap, per * p.cap)
        rows = arrived[at, :]
        out = expert_forward(p, rows, w_in, w_back)
        produced[at, :] = out
        ret_out[at, :] = (out * slot_gates(p, rows, pair[at, :].astype(F32), router[...])).astype(BF)
        for s in range(max(begin, 1), begin + per):
            back.append(slot_send(p, ret_out, ret_in, sems[2:4], s, slot_source(p, s)))
    ret_in[0 : p.cap, :] = ret_out[0 : p.cap, :]
    for copy in there_u:
        copy.wait_recv()
    pairs = pair[...].astype(F32)
    gate = slot_gates(p, arrived[...], pairs, router[...])
    u = u_in[...].astype(F32)
    grads[...] = (u * gate).astype(BF)
    dots = jnp.sum(u * produced[...], axis=-1, keepdims=True)
    expert_backward(
        p, arrived, grads, w_in, w_back, grad_w_in, grad_w_back, None, None, arrived_t, grad_rows
    )
    grad_router[...] = router_back(p, gate, dots, pairs, arrived[...], router[...], grad_rows)
    gret_out[...] = grad_rows[...].astype(BF)
    gret_in[0 : p.cap, :] = gret_out[0 : p.cap, :]
    back_g = [slot_send(p, gret_out, gret_in, sems[6:8], s, slot_source(p, s)) for s in range(1, p.experts)]
    for copy in back:
        copy.wait()
    second = middle[...] + mm(comb[...], ret_in[...])
    result[...] = (stop * first + (1.0 - stop) * second).astype(BF)
    grad_stop = jnp.sum(cot * (first - second), axis=-1, keepdims=True)
    coeff = grad_stop * stop * (1.0 - stop)
    grad_halt[...] = jnp.sum(coeff * first, axis=0, keepdims=True)
    grad_first[...] = stop * cot + coeff * halt[...]
    for copy in back_g:
        copy.wait()
    for copy in list(there.values()) + there_u:
        copy.wait_send()
    grad_middle[...], grad_gain[...] = norm_two_back(
        middle, gain_two, mm(comb[...], gret_in[...]), (1.0 - stop) * cot
    )


def expert_backward_kernel(
    p, g_ref, middle, gain_two, gain_before, disp, comb, pair, w_in, w_back, router, arrived, produced,
    before_in, before_back, before_router,
    grad_middle, grad_gain, grad_w_in, grad_w_back, grad_router,
    u_out, u_in, gret_out, gret_in, arrived_t, grads, grad_rows, *sems,
):
    greet(slot_peers(p))
    u_out[...] = mm(disp[...], g_ref[...].astype(BF)).astype(BF)
    u_in[0 : p.cap, :] = u_out[0 : p.cap, :]
    there = [slot_send(p, u_out, u_in, sems[0:2], s, slot_peer(p, s)) for s in range(1, p.experts)]
    pairs = pair[...].astype(F32)
    gate = slot_gates(p, arrived[...], pairs, router[...])
    for copy in there:
        copy.wait_recv()
    u = u_in[...].astype(F32)
    grads[...] = (u * gate).astype(BF)
    dots = jnp.sum(u * produced[...].astype(F32), axis=-1, keepdims=True)
    expert_backward(
        p, arrived, grads, w_in, w_back, grad_w_in, grad_w_back, before_in, before_back, arrived_t, grad_rows
    )
    grad_router[...] = before_router[...] + router_back(p, gate, dots, pairs, arrived[...], router[...], grad_rows)
    gret_out[...] = grad_rows[...].astype(BF)
    gret_in[0 : p.cap, :] = gret_out[0 : p.cap, :]
    back = [slot_send(p, gret_out, gret_in, sems[2:4], s, slot_source(p, s)) for s in range(1, p.experts)]
    for copy in back:
        copy.wait()
    for copy in there:
        copy.wait_send()
    grad_middle[...], gain = norm_two_back(middle, gain_two, mm(comb[...], gret_in[...]), g_ref[...])
    grad_gain[...] = gain_before[...] + gain


def sums_kernel(
    p, grad_w, grad_in, grad_back, small, out_w, out_in, out_back, out_small,
    w_out1, w_in1, w_out2, w_in2, in_out1, in_in1, in_out2, in_in2, bk_out1, bk_in1, bk_out2, bk_in2, all_small, *sems,
):
    b, d = place()
    z, x = d // p.lo, lax.rem(d, p.lo)
    y, c = b // 2, lax.rem(b, 2)
    e, g = b // p.group, lax.rem(b, p.group)
    greet(pack_peers(p) + dp_peers(p) + expert_peers(p))
    rows = out_w.shape[0]
    in_rows, back_rows = out_in.shape[1], out_back.shape[1]
    lo, hi, near, wide, tiny = (sems[2 * k : 2 * k + 2] for k in range(5))

    def rows_of(ref, index, size):
        return ref[pl.ds(aligned(index * size, size), size), :]

    near_copies = {}
    for k in range(p.local):
        to = turn(e, k + 1, p.local)
        for t in range(1, p.group):
            member = turn(g, t, p.group)
            slot = k * (p.group - 1) + t - 1
            in_out1[slot] = rows_of(grad_in, to * p.group + member, in_rows).astype(BF)
            bk_out1[slot] = rows_of(grad_back, to * p.group + member, back_rows).astype(BF)
            peer = (e * p.group + member, d)
            near_copies[k, t] = [
                send(in_out1.at[slot], in_in1.at[slot], near, 2 * slot, peer),
                send(bk_out1.at[slot], bk_in1.at[slot], near, 2 * slot + 1, peer),
            ]
    lo_copies = {}
    for k in range(p.hi):
        to = turn(z, k + 1, p.hi)
        for t in range(1, p.lo):
            slot = k * (p.lo - 1) + t - 1
            xx = turn(x, t, p.lo)
            w_out1[slot] = rows_of(grad_w, to * p.lo + xx, rows).astype(BF)
            lo_copies[k, t] = send(w_out1.at[slot], w_in1.at[slot], lo, slot, (b, z * p.lo + xx))
    wide_copies = []
    for k in range(p.local):
        to = turn(e, k + 1, p.local)
        for copies in [near_copies[k, t] for t in range(1, p.group)]:
            for copy in copies:
                copy.wait_recv()
        slots = [k * (p.group - 1) + t - 1 for t in range(1, p.group)]
        total_in = rows_of(grad_in, to * p.group + g, in_rows)
        total_back = rows_of(grad_back, to * p.group + g, back_rows)
        for slot in slots:
            total_in = total_in + in_in1[slot].astype(F32)
            total_back = total_back + bk_in1[slot].astype(F32)
        if k < p.local - 1:
            in_out2[k] = total_in.astype(BF)
            bk_out2[k] = total_back.astype(BF)
            peer = (to * p.group + g, d)
            wide_copies.append(send(in_out2.at[k], in_in2.at[k], wide, 2 * k, peer))
            wide_copies.append(send(bk_out2.at[k], bk_in2.at[k], wide, 2 * k + 1, peer))
        else:
            out_in[e] = total_in
            out_back[e] = total_back
    hi_copies = []
    total_w = None
    for k in range(p.hi):
        to = turn(z, k + 1, p.hi)
        for t in range(1, p.lo):
            lo_copies[k, t].wait_recv()
        total = rows_of(grad_w, to * p.lo + x, rows)
        for t in range(1, p.lo):
            total = total + w_in1[k * (p.lo - 1) + t - 1].astype(F32)
        if k < p.hi - 1:
            w_out2[k] = total.astype(BF)
            hi_copies.append(send(w_out2.at[k], w_in2.at[k], hi, k, (b, to * p.lo + x)))
        else:
            total_w = total
    current = small[...]
    tiny_copies = []
    sem = 0
    axes = (
        (2, c, lambda t: (2 * y + turn(c, t, 2), d)),
        (p.chips, y, lambda t: (2 * turn(y, t, p.chips) + c, d)),
        (p.lo, x, lambda t: (b, z * p.lo + turn(x, t, p.lo))),
        (p.hi, z, lambda t: (b, turn(z, t, p.hi) * p.lo + x)),
    )
    base = 0
    for size, index, peer in axes:
        all_small[base + index] = current
        copies = []
        for t in range(1, size):
            at = all_small.at[base + index]
            copies.append(send(at, at, tiny, sem, peer(t)))
            sem += 1
        for copy in copies:
            copy.wait_recv()
        current = all_small[base]
        for k in range(1, size):
            current = current + all_small[base + k]
        base += size
        tiny_copies += copies
    out_small[...] = current
    for k, copy in enumerate(hi_copies):
        copy.wait_recv()
        total_w = total_w + w_in2[k].astype(F32)
    out_w[...] = total_w
    for copy in wide_copies:
        copy.wait_recv()
    for k in range(p.local - 1):
        source = turn(e, -(k + 1), p.local)
        out_in[source] = in_in2[k].astype(F32)
        out_back[source] = bk_in2[k].astype(F32)
    for copies in near_copies.values():
        for copy in copies:
            copy.wait_send()
    for copy in list(lo_copies.values()) + wide_copies + hi_copies + tiny_copies:
        copy.wait_send()


def dma_pairs(*sizes):
    return [pltpu.SemaphoreType.DMA((max(1, size),)) for size in sizes for _ in range(2)]


def call(kernel, name, number, outs, ins, scratch, any_in=(), any_out=()):
    vmem = pl.BlockSpec(memory_space=pltpu.VMEM)
    anywhere = pl.BlockSpec(memory_space=pl.ANY)
    return pl.pallas_call(
        kernel,
        out_shape=tuple(jax.ShapeDtypeStruct(shape, dtype) for shape, dtype in outs),
        in_specs=[anywhere if k in any_in else vmem for k in range(len(ins))],
        out_specs=tuple(anywhere if k in any_out else vmem for k in range(len(outs))),
        scratch_shapes=scratch,
        compiler_params=pltpu.CompilerParams(
            collective_id=number, has_side_effects=True, vmem_limit_bytes=VMEM_BYTES
        ),
        name=name,
    )(*ins)


def on_device(
    inputs,
    segments,
    attention_routes,
    expert_routes,
    gain_mixer,
    gain_expert,
    weight_query,
    weight_key,
    weight_value,
    weight_out,
    router_mixer,
    router_expert,
    weight_in,
    weight_back,
    halt_weight,
    cotangent,
):
    blk, dp = lax.axis_size("blk"), lax.axis_size("dp")
    seq, width = inputs.shape[1:]
    experts, local = router_expert.shape[1], weight_in.shape[0]
    slots_of = max(2, 3 * seq // experts)
    hi = 4
    p = Plan(
        blk=blk,
        dp=dp,
        lo=dp // hi,
        hi=hi,
        seq=seq,
        width=width,
        heads=HEADS // blk,
        mixers=weight_query.shape[0],
        top=attention_routes.shape[-1],
        experts=experts,
        local=local,
        group=blk // local,
        cap=-(-slots_of // 16) * 16,
        ff=weight_in.shape[2],
    )
    cols, length, blocks, top = p.cols, p.length, p.blocks, p.top
    share = weight_key.shape[0]

    wall = jnp.concatenate(
        [
            jnp.transpose(weight_query, (1, 0, 2)).reshape(share, p.mixers * cols),
            weight_key,
            weight_value,
            jnp.transpose(weight_out, (2, 0, 1)).reshape(share, p.mixers * cols),
        ],
        axis=1,
    )
    picks = jnp.transpose(attention_routes[:, 0], (0, 2, 1)).reshape(2 * top, seq)
    routes = jnp.transpose(expert_routes[:, 0], (0, 2, 1)).reshape(-1, seq)
    seg_rows = segments.reshape(1, length)
    seg_cols = jnp.pad(segments[0], (MAXLEN, 0), constant_values=-1).reshape(length + MAXLEN, 1)
    gain_one = gain_mixer.astype(F32).reshape(1, width)
    gain_two = gain_expert.astype(F32).reshape(1, width)
    halt = halt_weight.astype(F32).reshape(1, width)
    router_row = router_mixer.T
    router = jnp.pad(router_expert, ((0, 0), (0, LANES - experts)))
    start = inputs[0].astype(F32)

    all_w, all_in, all_back, all_picks, disp, comb, _, pair = call(
        functools.partial(setup_kernel, p),
        "setup",
        0,
        [
            ((width, p.all_cols), BF),
            ((width, p.ff), BF),
            ((p.ff, width), BF),
            ((blk, 2 * top, seq), jnp.int32),
            ((2, p.slots, seq), BF),
            ((2, seq, p.slots), BF),
            ((2, p.slots, LANES), BF),
            ((2, p.slots, LANES), BF),
        ],
        [wall, weight_in, weight_back, picks, routes],
        dma_pairs(
            p.hi - 1,
            p.hi * (p.lo - 1),
            2 * (p.local - 1),
            2 * p.local * (p.group - 1),
        )
        + pack_sems(p)
        + dma_pairs(2 * p.experts)
        + [pltpu.SemaphoreType.DMA((3,))],
        any_in=(0, 1, 2),
        any_out=(0, 1, 2),
    )

    def pack_scratch():
        return [
            pltpu.VMEM((blk, width, seq), BF),
            pltpu.VMEM((width, seq), F32),
            pltpu.VMEM((p.chips, width, seq), BF),
            pltpu.VMEM((max(1, p.chips - 1), width, seq), BF),
            pltpu.VMEM((max(1, p.chips - 1), width, seq), BF),
        ] + pack_sems(p) * 2

    def attention_forward(state, step):
        return call(
            functools.partial(attention_forward_kernel, p, step),
            f"attention_forward_{step}",
            1 + step,
            [
                ((seq, width), F32),
                ((seq, width), BF),
                ((blk, width, seq), BF),
                ((blocks, cols, top * QROWS), BF),
                ((cols, length + MAXLEN), BF),
                ((cols, length + MAXLEN), BF),
                ((blocks, 8, top * QROWS), F32),
                ((blocks, cols, top * QROWS), BF),
                ((p.mixers * cols, length), BF),
                ((blk, 8, seq), F32),
            ],
            [state, gain_one, gain_two, all_w, router_row, all_picks, seg_rows, seg_cols],
            [
                pltpu.VMEM((p.qkv, width), BF),
                pltpu.VMEM((p.heads, length + MAXLEN, cols), BF),
            ]
            + pack_scratch(),
        )

    def attention_backward(grad, base, state, saved, step, before):
        ins = [grad, base, state, gain_one, all_w, router_mixer, all_picks, seg_rows, seg_cols, *saved]
        return call(
            functools.partial(attention_backward_kernel, p, step, before is None),
            f"attention_backward_{step}",
            3 + step,
            [
                ((seq, width), F32 if before is None else BF),
                ((width, p.all_cols), F32),
                ((p.mixers, width), F32),
                ((1, width), F32),
            ],
            ins + ([] if before is None else list(before)),
            [
                pltpu.VMEM((blk, width, seq), BF),
                pltpu.VMEM((p.mixers * cols, width), BF),
                pltpu.VMEM((p.heads, length + MAXLEN, cols), BF),
                pltpu.VMEM((p.heads, length + MAXLEN, cols), BF),
                pltpu.VMEM((blocks, cols, top * QROWS), BF),
                pltpu.VMEM((blk, p.mixers, seq), F32),
                pltpu.VMEM((cols, length + MAXLEN), F32),
                pltpu.VMEM((cols, length + MAXLEN), F32),
                pltpu.VMEM((p.qkv, length), BF),
            ]
            + pack_scratch(),
        )

    rows_bf = pltpu.VMEM((p.slots, width), BF)
    rows_f = pltpu.VMEM((p.slots, width), F32)
    cols_bf = pltpu.VMEM((width, p.slots), BF)

    middle0, m0, *saved0 = attention_forward(start, 0)
    first, arrived0, produced0 = call(
        functools.partial(expert_forward_kernel, p),
        "expert_forward",
        5,
        [((seq, width), F32), ((p.slots, width), BF), ((p.slots, width), BF)],
        [m0, middle0, disp[0], comb[0], pair[0], all_in, all_back, router],
        [rows_bf] * 3 + dma_pairs(p.experts, p.experts),
    )
    middle1, m1, *saved1 = attention_forward(first, 1)
    result, grad_first, grad_middle1, gain_two1, grad_halt, in1, back1, router1 = call(
        functools.partial(expert_both_kernel, p),
        "expert_both",
        6,
        [
            ((seq, width), BF),
            ((seq, width), F32),
            ((seq, width), F32),
            ((1, width), F32),
            ((1, width), F32),
            ((width, p.ff), F32),
            ((p.ff, width), F32),
            ((LANES, width), F32),
        ],
        [m1, middle1, first, cotangent[0], halt, gain_two, disp[1], comb[1], pair[1], all_in, all_back, router],
        [rows_bf] * 8
        + [cols_bf, rows_bf, rows_f, rows_f]
        + dma_pairs(p.experts, p.experts, p.experts, p.experts),
    )
    grad_first, w1, mixer1, gain_one1 = attention_backward(grad_middle1, grad_first, first, saved1, 1, None)
    grad_middle0, grad_gain_two, grad_in, grad_back, grad_router = call(
        functools.partial(expert_backward_kernel, p),
        "expert_backward",
        7,
        [
            ((seq, width), F32),
            ((1, width), F32),
            ((width, p.ff), F32),
            ((p.ff, width), F32),
            ((LANES, width), F32),
        ],
        [
            grad_first, middle0, gain_two, gain_two1, disp[0], comb[0], pair[0], all_in, all_back, router,
            arrived0, produced0, in1, back1, router1,
        ],
        [rows_bf] * 4 + [cols_bf, rows_bf, rows_f] + dma_pairs(p.experts, p.experts),
    )
    input_grad, grad_w, grad_mixer, grad_gain_one = attention_backward(
        grad_middle0, grad_middle0, start, saved0, 0, (w1, mixer1, gain_one1)
    )
    small = jnp.concatenate(
        [
            grad_gain_one,
            grad_gain_two,
            grad_halt,
            jnp.zeros((5, width), F32),
            grad_mixer,
            grad_router[:experts],
        ]
    )
    in_rows, back_rows = weight_in.shape[1], weight_back.shape[1]
    near = p.local * (p.group - 1)
    far = max(1, p.local - 1)
    out_w, out_in, out_back, small = call(
        functools.partial(sums_kernel, p),
        "sums",
        8,
        [
            ((share, p.all_cols), F32),
            ((local, in_rows, p.ff), F32),
            ((local, back_rows, width), F32),
            (small.shape, F32),
        ],
        [grad_w, grad_in, grad_back, small],
        [pltpu.VMEM((p.hi * (p.lo - 1), share, p.all_cols), BF)] * 2
        + [pltpu.VMEM((p.hi - 1, share, p.all_cols), BF)] * 2
        + [pltpu.VMEM((near, in_rows, p.ff), BF)] * 2
        + [pltpu.VMEM((far, in_rows, p.ff), BF)] * 2
        + [pltpu.VMEM((near, back_rows, width), BF)] * 2
        + [pltpu.VMEM((far, back_rows, width), BF)] * 2
        + [pltpu.VMEM((2 + p.chips + p.lo + p.hi, *small.shape), F32)]
        + dma_pairs(
            p.hi * (p.lo - 1),
            p.hi - 1,
            2 * near,
            2 * (p.local - 1),
            2 + p.chips + p.lo + p.hi,
        ),
    )
    q_cols = p.mixers * cols
    query = jnp.transpose(out_w[:, :q_cols].reshape(share, p.mixers, cols), (1, 0, 2))
    out = jnp.transpose(out_w[:, p.qkv :].reshape(share, p.mixers, cols), (1, 2, 0))
    return (
        result[None],
        input_grad[None],
        small[0],
        small[1],
        query,
        out_w[:, q_cols : q_cols + cols],
        out_w[:, q_cols + cols : p.qkv],
        out,
        small[8 : 8 + p.mixers].T,
        small[8 + p.mixers :].T,
        out_in,
        out_back,
        small[2],
    )


def solution(mesh):
    return jax.shard_map(
        on_device,
        mesh=mesh,
        in_specs=(
            P("dp", "blk", None),
            P("dp", None),
            P(None, "dp", "blk", None),
            P(None, "dp", "blk", None),
            P(),
            P(),
            P(None, "dp", "blk"),
            P("dp", "blk"),
            P("dp", "blk"),
            P(None, "blk", "dp"),
            P(),
            P(),
            P("dp", "blk", None),
            P("dp", "blk", None),
            P(),
            P("dp", "blk", None),
        ),
        out_specs=(
            P("dp", "blk", None),
            P("dp", "blk", None),
            P(),
            P(),
            P(None, "dp", "blk"),
            P("dp", "blk"),
            P("dp", "blk"),
            P(None, "blk", "dp"),
            P(),
            P(),
            P("dp", "blk", None),
            P("dp", "blk", None),
            P(),
        ),
        check_vma=False,
    )
```

time: 1180 us -> 489 us (0.41)
  Pallas kernels: 0 us -> 453 us
  waiting for transfers between devices: 452 us -> 0 us
  matrix products: 255 us -> 0 us
  blocking collectives: 186 us -> 0 us
  local copies, waits for them, and re-layouts: 149 us -> 27.1 us
  other arithmetic: 75 us -> 4.07 us
  starting transfers between devices: 40.1 us -> 0 us
  between operations: 17.5 us -> 1.13 us
    pallas_call x0 -> x9, Pallas kernels: none -> 453 us  [call(): pl.pallas_call(kernel, out_shape=tuple((jax.ShapeDtypeStruct(shape, dtype...]
    reduce_scatter x6 -> x0, waiting for transfers between devices: 271 us -> none  [the longest x1 78 us: on_device(): lax.psum_scatter(grad_query_w.astype(jnp.bfloat16), 'dp', scatter_dimensi...]
    dot_general x82 -> x0, matrix products: 255 us -> none  [the longest x2 34.6 us: step_forward(): jnp.einsum('sxcd,xdf->sxcf', arrived, local_in, preferred_element_type=jn...]
    all_gather x6 -> x0, blocking collectives: 96.7 us -> none  [the longest x1 33.6 us: on_device(): lax.all_gather(full_key, 'dp', axis=0, tiled=True)]
    all_to_all x6 -> x0, waiting for transfers between devices: 68.8 us -> none  [the longest x2 31.6 us: step_forward(): lax.all_to_all(produced, 'dp', split_axis=0, concat_axis=0, tiled=True)]
    all_gather x4 -> x0, waiting for transfers between devices: 65.9 us -> none  [the longest x1 25.7 us: on_device(): lax.all_gather(full_out, 'dp', axis=2, tiled=True)]
    all_to_all x2 -> x0, blocking collectives: 46.8 us -> none  [the longest x1 23.6 us: step_backward(): lax.all_to_all(grad_outgoing, 'dp', split_axis=0, concat_axis=0, tiled=True)]
    unnamed x18 -> x0, waiting for transfers between devices: 44.5 us -> none
  transfers between devices with their start and end apart: 28 -> 0, of which waited for: 17 -> 0; matrix products, arithmetic and copies ran while one was open for 23% -> 0% of each run, Pallas kernels for 0% -> 0%
where the time goes in v1:
time: 489 us; the launch traced here: 486 us
  Pallas kernels  453 us (93%)
  local copies, waits for them, and re-layouts  27.1 us (6%)
    pallas_call x9, Pallas kernels, call(): pl.pallas_call(kernel, out_shape=tuple((jax.ShapeDtypeStruct(shape, dtype...  453 us

profile of v1, /device:TPU:0, one launch (start us, length us, event | category | flops | bytes accessed | tf_op | source)
XLA Modules:
  0.0 485.7 jit_solution(840148796410001770)
XLA Ops:
  1.6 0.9 copy_bitcast_fusion
  2.5 1.5 pad_maximum_fusion.wall
  4.0 1.3 reshape.70.picks
  5.3 1.3 reshape.71.routes
  6.6 51.7 %setup.1 = (bf16[512,2304]{1,0:T(8,128)(2,1)}, bf16[512,2048]{1,0:T(8,128)(2,1)}, bf16[2048,512]{1,0:T(8,128)(2,1)}, s32[4,8,256]{2,1,0:T(8,128)}, bf16[2,768,25...) custom-call(bf16[64,2304]{1,0:T(8,128)(2,1)} %pad_maximum_fusion.wal, ...), custom_call_target="tpu_custom_call" | custom-call | tf_op jit(solution)/shard_map/setup/pallas_call | solution.py:864
  58.3 1.1 reshape.84.seg_cols
  61.4 37.3 %attention_forward_0.1 = (f32[256,512]{1,0:T(8,128)}, bf16[256,512]{1,0:T(8,128)(2,1)}, bf16[4,512,256]{2,1,0:T(8,128)(2,1)}, bf16[8,128,512]{2,1,0:T(8,128)(2,1...) custom-call(f32[256,512]{1,0:T(8,128)} %bitcast_convert_fusion.h_ref, ...), custom_call_target="tpu_custom_call" | custom-call | tf_op jit(solution)/shard_map/attention_forward_0/pallas_call | solution.py:864
  98.7 1.0 slice_bitcast_fusion
  102.2 48.4 %expert_forward.1 = (f32[256,512]{1,0:T(8,128)}, bf16[768,512]{1,0:T(8,128)(2,1)}, bf16[768,512]{1,0:T(8,128)(2,1)}) custom-call(bf16[256,512]{1,0:T(8,128)(2,1)} %get-tuple-element.70.m_ref, f32[256,512]{1,0:T(8,128)} %get-tuple-element.71.middle, bf16[768,256]{1,0:T(8,128)(2,1)} %get-tuple-element.126.disp, bf16[256,768]{1,0:T(8,128)(2,1)} %get-tuple-element.124.comb, ...), custom_call_target="tpu_custom_call" | custom-call | tf_op jit(solution)/shard_map/expert_forward/pallas_call | solution.py:864
  150.7 37.3 %attention_forward_1.1 = (f32[256,512]{1,0:T(8,128)}, bf16[256,512]{1,0:T(8,128)(2,1)}, bf16[4,512,256]{2,1,0:T(8,128)(2,1)}, bf16[8,128,512]{2,1,0:T(8,128)(2,1...) custom-call(f32[256,512]{1,0:T(8,128)} %get-tuple-element.77.h_ref.f, ...), custom_call_target="tpu_custom_call" | custom-call | tf_op jit(solution)/shard_map/attention_forward_1/pallas_call | solution.py:864
  188.6 82.2 %expert_both.1 = (bf16[256,512]{1,0:T(8,128)(2,1)}, f32[256,512]{1,0:T(8,128)}, f32[256,512]{1,0:T(8,128)}, f32[1,512]{1,0:T(1,128)}, f32[1,512]{1,0:T(1,128)}, ...) custom-call(bf16[256,512]{1,0:T(8,128)(2,1)} %get-tuple-element.78.m_ref, ...), custom_call_target="tpu_custom_call" | custom-call | tf_op jit(solution)/shard_map/expert_both/pallas_call | solution.py:864
  271.5 42.6 %attention_backward_1.1 = (f32[256,512]{1,0:T(8,128)}, f32[512,2304]{1,0:T(8,128)}, f32[8,512]{1,0:T(8,128)}, f32[1,512]{1,0:T(1,128)}) custom-call(f32[256,512]{1,0:T(8,128)} %get-tuple-element.81.grad_ref, f32[256,512]{1,0:T(8,128)} %get-tuple-element.82.base_ref, f32[256,512]{1,0:T(8,128)} %get-tuple-element.77.h_ref.first_ref, f32[1,512]{1,0:T(1,128)} %bitcast.78, ...), custom_call_target="tpu_custom_call" | custom-call | tf_op jit(solution)/shard_map/attention_backward_1/pallas_call | solution.py:864
  314.2 59.2 %expert_backward.1 = (f32[256,512]{1,0:T(8,128)}, f32[1,512]{1,0:T(1,128)}, f32[512,2048]{1,0:T(8,128)}, f32[2048,512]{1,0:T(8,128)}, f32[128,512]{1,0:T(8,128)}) custom-call(f32[256,512]{1,0:T(8,128)} %get-tuple-element.91.g_ref, f32[256,512]{1,0:T(8,128)} %get-tuple-element.71.middle, f32[1,512]{1,0:T(1,128)} %bitcast.75, ...), custom_call_target="tpu_custom_call" | custom-call | tf_op jit(solution)/shard_map/expert_backward/pallas_call | solution.py:864
  373.4 44.0 %attention_backward_0.1 = (bf16[256,512]{1,0:T(8,128)(2,1)}, f32[512,2304]{1,0:T(8,128)}, f32[8,512]{1,0:T(8,128)}, f32[1,512]{1,0:T(1,128)}) custom-call(f32[256,512]{1,0:T(8,128)} %get-tuple-element.98.grad_ref.base_ref, f32[256,512]{1,0:T(8,128)} %get-tuple-element.98.grad_ref.base_ref, f32[256,512]{1,0:T(8,128)} %bitcast_convert_fusion.h_ref, ...), custom_call_target="tpu_custom_call" | custom-call | tf_op jit(solution)/shard_map/attention_backward_0/pallas_call | solution.py:864
  418.2 3.2 concatenate.7.small
  421.4 50.7 %sums.1 = (f32[64,2304]{1,0:T(8,128)}, f32[2,128,2048]{2,1,0:T(8,128)}, f32[2,512,512]{2,1,0:T(8,128)}, f32[32,512]{1,0:T(8,128)}) custom-call(f32[512,2304]{1,0:T(8,128)} %get-tuple-element.111.grad_w, f32[512,2048]{1,0:T(8,128)} %get-tuple-element.112.grad_in, f32[2048,512]{1,0:T(8,128)} %get-tuple-element.113.grad_back, f32[32,512]{1,0:T(8,128)} %concatenate.7.small), custom_call_target="tpu_custom_call" | custom-call | tf_op jit(solution)/shard_map/sums/pallas_call | solution.py:864
  472.2 1.2 slice_bitcast_fusion.4
  474.9 1.4 fusion
  476.3 1.4 slice_bitcast_fusion.8
  477.6 1.3 slice_bitcast_fusion.9
  479.0 1.4 fusion.1
  481.8 1.3 copy.63
  483.1 1.0 copy-done.2
  484.1 1.3 copy.64
  (51 shorter events, 10.4 us)
Async XLA Ops:
  0.6 0.9 copy-start
  0.7 57.6 %copy-start.10 = (s32[1,1024]{1,0:T(1,128)S(1)}, s32[1,1024]{1,0:T(1,128)}, u32[]{:S(2)}) copy-start(s32[1,1024]{1,0:T(1,128)} %seg_rows.7) | copy-start | bytes 12292
  0.7 58.7 %copy-start.15 = (bf16[512]{0:T(512)(128)(2,1)S(1)}, bf16[512]{0:T(512)(128)(2,1)}, u32[]{:S(2)}) copy-start(bf16[512]{0:T(512)(128)(2,1)} %param.20) | copy-start | bytes 3076
  0.7 59.3 %copy-start.16 = (bf16[512]{0:T(512)(128)(2,1)S(1)}, bf16[512]{0:T(512)(128)(2,1)}, u32[]{:S(2)}) copy-start(bf16[512]{0:T(512)(128)(2,1)} %param.21) | copy-start | bytes 3076
  0.7 59.9 %copy-start.7 = (bf16[1,256,512]{2,1,0:T(8,128)(2,1)S(1)}, bf16[1,256,512]{2,1,0:T(8,128)(2,1)}, u32[]{:S(2)}) copy-start(bf16[1,256,512]{2,1,0:T(8,128)(2,1)} %param.16) | copy-start | bytes 786436
  60.6 38.2 %copy-start.5 = (bf16[2,256,768]{2,1,0:T(8,128)(2,1)S(1)}, bf16[2,256,768]{2,1,0:T(8,128)(2,1)}, u32[]{:S(2)}) copy-start(bf16[2,256,768]{2,1,0:T(8,128)(2,1)} %get-tuple-element.73) | copy-start | bytes 2359300
  61.4 38.3 %copy-start.4 = (bf16[2,768,256]{2,1,0:T(8,128)(2,1)S(1)}, bf16[2,768,256]{2,1,0:T(8,128)(2,1)}, u32[]{:S(2)}) copy-start(bf16[2,768,256]{2,1,0:T(8,128)(2,1)} %get-tuple-element.72) | copy-start | bytes 2359300
  98.7 1.9 copy-start.6
  98.7 2.7 copy-start.12
  150.7 37.3 %copy-start.17 = (bf16[512]{0:T(512)(128)(2,1)S(1)}, bf16[512]{0:T(512)(128)(2,1)}, u32[]{:S(2)}) copy-start(bf16[512]{0:T(512)(128)(2,1)} %param.30) | copy-start | bytes 3076
  188.6 82.2 %copy-start.11 = (bf16[512,8]{0,1:T(8,128)(2,1)S(1)}, bf16[512,8]{0,1:T(8,128)(2,1)}, u32[]{:S(2)}) copy-start(bf16[512,8]{0,1:T(8,128)(2,1)} %param.26) | copy-start | bytes 24580
  373.4 44.8 %copy-start.13 = (f32[1,512]{1,0:T(1,128)S(1)}, f32[1,512]{1,0:T(1,128)}, u32[]{:S(2)}) copy-start(f32[1,512]{1,0:T(1,128)} %get-tuple-element.116) | copy-start | bytes 6148
  373.4 44.8 %copy-start.14 = (f32[1,512]{1,0:T(1,128)S(1)}, f32[1,512]{1,0:T(1,128)}, u32[]{:S(2)}) copy-start(f32[1,512]{1,0:T(1,128)} %get-tuple-element.115) | copy-start | bytes 6148
  472.2 8.2 %copy-start.8 = (bf16[256,512]{1,0:T(8,128)(2,1)S(1)}, bf16[256,512]{1,0:T(8,128)(2,1)}, u32[]{:S(2)}) copy-start(bf16[256,512]{1,0:T(8,128)(2,1)} %get-tuple-element.80) | copy-start | bytes 786436
  472.2 8.9 %copy-start.9 = (bf16[256,512]{1,0:T(8,128)(2,1)S(1)}, bf16[256,512]{1,0:T(8,128)(2,1)}, u32[]{:S(2)}) copy-start(bf16[256,512]{1,0:T(8,128)(2,1)} %get-tuple-element.110) | copy-start | bytes 786436
  472.2 9.6 %copy-start.3 = (f32[2,128,2048]{2,1,0:T(8,128)S(1)}, f32[2,128,2048]{2,1,0:T(8,128)}, u32[]{:S(2)}) copy-start(f32[2,128,2048]{2,1,0:T(8,128)} %get-tuple-element.161) | copy-start | bytes 6291460
  481.8 2.3 copy-start.2
  481.8 3.7 copy-start.1

commit v2 on v0

v2 whole, which is shorter than its diff:
```python
import functools
from types import SimpleNamespace
from typing import NamedTuple

import jax
import jax.numpy as jnp
from jax import lax
from jax.experimental import pallas as pl
from jax.experimental.pallas import tpu as pltpu
from jax.sharding import PartitionSpec as P

HEADS = 8
HD = 64
MAXLEN = 256
QROWS = 128
WINDOW = MAXLEN + QROWS
LANES = 128
EPSILON = 1e-06
MASKED_SCORE = -1e30
MESH = pl.DeviceIdType.MESH
BF = jnp.bfloat16
F32 = jnp.float32
VMEM_BYTES = 61 * 2**20


class Plan(NamedTuple):
    blk: int
    dp: int
    lo: int
    hi: int
    seq: int
    width: int
    heads: int
    mixers: int
    top: int
    experts: int
    local: int
    group: int
    cap: int
    ff: int

    @property
    def length(self):
        return self.blk * self.seq

    @property
    def cols(self):
        return self.heads * HD

    @property
    def qkv(self):
        return (self.mixers + 2) * self.cols

    @property
    def all_cols(self):
        return (2 * self.mixers + 2) * self.cols

    @property
    def blocks(self):
        return self.length // QROWS

    @property
    def slots(self):
        return self.experts * self.cap

    @property
    def tile(self):
        return 512 if self.slots <= 768 else 256

    @property
    def chips(self):
        return self.blk // 2


def mm(a, b):
    return lax.dot_general(a, b, (((1,), (0,)), ((), ())), preferred_element_type=F32)


def mm_nt(a, b):
    return lax.dot_general(a, b, (((1,), (1,)), ((), ())), preferred_element_type=F32)


def place():
    return lax.axis_index("blk"), lax.axis_index("dp")


def turn(index, by, size):
    return lax.rem(index + (by % size), size)


def greet(peers):
    barrier = pltpu.get_barrier_semaphore()
    for peer in peers:
        pl.semaphore_signal(barrier, inc=1, device_id=peer, device_id_type=MESH)
    pl.semaphore_wait(barrier, len(peers))


def send(src, dst, sems, slot, peer):
    copy = pltpu.make_async_remote_copy(
        src_ref=src,
        dst_ref=dst,
        send_sem=sems[0].at[slot],
        recv_sem=sems[1].at[slot],
        device_id=peer,
        device_id_type=MESH,
    )
    copy.start()
    return copy


def aligned(value, by):
    return pl.multiple_of(value, by)


def pack_peers(p):
    b, d = place()
    y, c = b // 2, lax.rem(b, 2)
    peers = [(2 * y + 1 - c, d)]
    return peers + [(2 * turn(y, s, p.chips) + c, d) for s in range(1, p.chips)]


def slot_peer(p, s):
    b, d = place()
    e, g = b // p.group, lax.rem(b, p.group)
    return (turn(e, s // p.dp, p.local) * p.group + g, turn(d, s % p.dp, p.dp))


def slot_peers(p):
    return [slot_peer(p, s) for s in range(1, p.experts)]


def slot_source(p, s):
    b, d = place()
    e, g = b // p.group, lax.rem(b, p.group)
    return (turn(e, -(s // p.dp), p.local) * p.group + g, turn(d, -(s % p.dp), p.dp))


def dp_peers(p):
    b, d = place()
    z, x = d // p.lo, lax.rem(d, p.lo)
    peers = [(b, turn(z, s, p.hi) * p.lo + x) for s in range(1, p.hi)]
    return peers + [(b, z * p.lo + turn(x, t, p.lo)) for t in range(1, p.lo)]


def expert_peers(p):
    b, d = place()
    e, g = b // p.group, lax.rem(b, p.group)
    peers = [(turn(e, s, p.local) * p.group + g, d) for s in range(1, p.local)]
    return peers + [(e * p.group + turn(g, t, p.group), d) for t in range(1, p.group)]


class PackGather:
    def __init__(self, p, buf, sems):
        self.p, self.buf, self.far, self.near = p, buf, sems[0:2], sems[2:4]
        self.done_near = self.done_far = False

    def begin(self):
        p = self.p
        b, d = place()
        y, c = b // 2, lax.rem(b, 2)
        own = self.buf.at[b]
        self.first = [
            send(own, own, self.far, s - 1, (2 * turn(y, s, p.chips) + c, d))
            for s in range(1, p.chips)
        ]
        self.second = [send(own, own, self.near, 0, (2 * y + 1 - c, d))]

    def finish_near(self):
        if not self.done_near:
            self.second[0].wait_recv()
        self.done_near = True

    def finish_far(self):
        if self.done_far:
            return
        self.done_far = True
        p = self.p
        b, d = place()
        y, c = b // 2, lax.rem(b, 2)
        for s in range(1, p.chips):
            self.first[s - 1].wait_recv()
            block = self.buf.at[2 * turn(y, -s, p.chips) + c]
            self.second.append(send(block, block, self.near, s, (2 * y + 1 - c, d)))
        self.finish_near()
        for copy in self.second[1:]:
            copy.wait_recv()

    def end(self):
        for copy in self.first + self.second:
            copy.wait_send()


class PackSum:
    def __init__(self, p, bufs, sems):
        self.p, self.bufs = p, bufs
        self.far, self.near = sems[0:2], sems[2:4]
        self.first, self.second = {}, []

    def give(self, s, term):
        p, r = self.p, self.bufs
        b, d = place()
        y, c = b // 2, lax.rem(b, 2)
        r.part[s] = term.astype(BF)
        self.first[s] = send(r.part.at[s], r.near_in.at[s], self.near, s, (2 * y + 1 - c, d))

    def pass_on(self, s, term):
        p, r = self.p, self.bufs
        b, d = place()
        y, c = b // 2, lax.rem(b, 2)
        self.first[s].wait_recv()
        r.far_out[s - 1] = (term + r.near_in[s].astype(F32)).astype(BF)
        self.second.append(
            send(r.far_out.at[s - 1], r.far_in.at[s - 1], self.far, s - 1, (2 * turn(y, s, p.chips) + c, d))
        )

    def total(self, term):
        r = self.bufs
        self.first[0].wait_recv()
        term = term + r.near_in[0].astype(F32)
        for k, copy in enumerate(self.second):
            copy.wait_recv()
            term = term + r.far_in[k].astype(F32)
        for copy in list(self.first.values()) + self.second:
            copy.wait_send()
        return term


def slot_send(p, src, dst, sems, s, peer):
    rows = pl.ds(s * p.cap, p.cap)
    return send(src.at[rows], dst.at[rows], sems, s, peer)


def slot_sends(p, src, dst, sems, peer):
    dst[0 : p.cap, :] = src[0 : p.cap, :]
    return {s: slot_send(p, src, dst, sems, s, peer(p, s)) for s in range(1, p.experts)}


def receive(copies, sources):
    for s in sources:
        if s in copies:
            copies[s].wait_recv()


def sent(copies):
    for copy in copies.values() if isinstance(copies, dict) else copies:
        copy.wait_send()


def move(r, src, dst):
    copy = pltpu.make_async_copy(src, dst, r.moves.at[r.moved])
    r.moved += 1
    copy.start()
    return copy


def moves(r, pairs):
    return [move(r, src, dst) for src, dst in pairs]


def arrive(copies):
    for copy in copies:
        copy.wait()
    copies.clear()


def norm_parts(state):
    inverse = lax.rsqrt(jnp.mean(state * state, axis=-1, keepdims=True) + EPSILON)
    return inverse, state * inverse


def norm_back(state, gain, grad):
    inverse, unit = norm_parts(state)
    scaled = grad * gain
    back = inverse * scaled - state * (inverse * inverse * inverse) * jnp.mean(
        scaled * state, axis=-1, keepdims=True
    )
    return back, jnp.sum(grad * unit, axis=0, keepdims=True)


def segment_columns(p, segments, seg_cols):
    seg_cols[0:MAXLEN, :] = jnp.full((MAXLEN, 8), -1.0, F32)
    for start in range(0, p.length, QROWS):
        row = segments[:, start : start + QROWS].astype(F32)
        seg_cols[MAXLEN + start : MAXLEN + start + QROWS, :] = jnp.broadcast_to(row, (8, QROWS)).T


def attention_mask(r, start):
    keys = r.seg_cols[pl.ds(start, WINDOW), 0:1]
    queries = r.segments[:, pl.ds(start, QROWS)].astype(F32)
    key_at = lax.broadcasted_iota(jnp.int32, (WINDOW, QROWS), 0) - MAXLEN
    query_at = lax.broadcasted_iota(jnp.int32, (WINDOW, QROWS), 1)
    return jnp.where((key_at <= query_at) & (keys == queries), 0.0, MASKED_SCORE)


def head_rows(p, dst, at, values):
    flat = values.T
    lane = lax.broadcasted_iota(jnp.int32, flat.shape, 1) // HD
    for h in range(p.heads):
        dst[h, at, :] = jnp.where(lane == h, flat, 0.0).astype(BF)


def pick_rows(p, routes, terms):
    picked = []
    for j in range(p.top):
        row = routes[j : j + 1, :]
        total = None
        for e in range(p.mixers):
            term = jnp.where(row == e, terms(e), 0.0)
            total = term if total is None else total + term
        picked.append(total)
    return picked


def spread_rows(p, routes, values, e):
    total = None
    for j in range(p.top):
        term = jnp.where(routes[j : j + 1, :] == e, values[j], 0.0)
        total = term if total is None else total + term
    return total


def pick_table(p, r, step, bb):
    return r.all_picks[bb, 8 * step : 8 * step + p.top, :]


def transposed(dst, src, rows, first, tile):
    for start in range(0, rows, tile):
        dst[start : start + tile, :] = src[:, first + start : first + start + tile].astype(F32).T.astype(BF)


def project(p, r, a, step, bb):
    cols, sub = p.cols, p.seq // QROWS
    states = a.nt[bb]
    table = pick_table(p, r, step, bb)
    logits = mm(r.router_row[...], states)
    chosen = pick_rows(p, table, lambda e: logits[e : e + 1, :])
    peak = functools.reduce(jnp.maximum, chosen)
    chosen = [jnp.exp(row - peak) for row in chosen]
    scale = 1.0 / sum(chosen)
    for j in range(p.top):
        a.gates[bb, j : j + 1, :] = chosen[j] * scale
    values = mm(r.w_t[...], states)
    for k in range(sub):
        lanes = slice(k * QROWS, (k + 1) * QROWS)
        queries = pick_rows(p, table[:, lanes], lambda e: values[e * cols : (e + 1) * cols, lanes])
        for j in range(p.top):
            a.qs[bb * sub + k, :, j * QROWS : (j + 1) * QROWS] = (queries[j] * (HD**-0.5)).astype(BF)
    at = pl.ds(aligned(MAXLEN + bb * p.seq, QROWS), p.seq)
    keys = values[p.mixers * cols : (p.mixers + 1) * cols, :]
    a.kt[:, at] = keys.astype(BF)
    a.vt[:, at] = values[(p.mixers + 1) * cols :, :].astype(BF)
    head_rows(p, r.k_heads, at, keys)


def attend(p, r, a, step, bb):
    cols, sub = p.cols, p.seq // QROWS

    @pl.loop(0, sub)
    def _(k):
        i = bb * sub + k
        start = aligned(i * QROWS, QROWS)
        keys = pl.ds(start, WINDOW)
        bias = attention_mask(r, start)
        bias = jnp.concatenate([bias] * p.top, axis=1)
        queries = a.qs[i]
        for head in range(p.heads):
            scores = mm(r.k_heads[head, keys, :], queries) + bias
            peak = jnp.max(scores, axis=0, keepdims=True)
            scores = jnp.exp(scores - peak)
            total = jnp.sum(scores, axis=0, keepdims=True)
            a.lse[i, head : head + 1, :] = peak + jnp.log(total)
            probs = (scores * (1.0 / total)).astype(BF)
            rows = slice(head * HD, (head + 1) * HD)
            a.att[i, rows, :] = mm(a.vt[rows, keys], probs).astype(BF)
        at = pl.ds(aligned(k * QROWS, QROWS), QROWS)
        table = r.all_picks[bb, 8 * step : 8 * step + p.top, at]
        weights = a.gates[bb, 0 : p.top, at]
        values = [
            a.att[i, :, j * QROWS : (j + 1) * QROWS].astype(F32) * weights[j : j + 1, :] for j in range(p.top)
        ]
        for e in range(p.mixers):
            a.mix[e * cols : (e + 1) * cols, pl.ds(start, QROWS)] = spread_rows(p, table, values, e).astype(BF)


def attention_forward(p, r, a, step, state, before, out_ready, after):
    b, _ = place()
    y, c = b // 2, lax.rem(b, 2)
    a.nt[b] = (norm_parts(state)[1] * r.gain_one[...]).T.astype(BF)
    gather = PackGather(p, a.nt, a.gather_sems)
    gather.begin()
    r.k_heads[:, 0:MAXLEN, :] = jnp.zeros((p.heads, MAXLEN, p.cols), BF)
    a.kt[:, 0:MAXLEN] = jnp.zeros((p.cols, MAXLEN), BF)
    a.vt[:, 0:MAXLEN] = jnp.zeros((p.cols, MAXLEN), BF)
    before(gather)
    project(p, r, a, step, b)
    gather.finish_near()
    project(p, r, a, step, 2 * y + 1 - c)
    attend(p, r, a, step, 2 * y + 1)
    gather.finish_far()
    for s in range(1, p.chips):
        yy = turn(y, s, p.chips)

        @pl.loop(0, 2)
        def _(k):
            project(p, r, a, step, 2 * yy + k)

    def branch(bb):
        return mm(r.all_w[:, p.qkv :], a.mix[:, pl.ds(aligned(bb * p.seq, p.seq), p.seq)])

    shares = PackSum(p, r, a.sum_sems)
    for s in range(1, p.chips):
        yy = turn(y, s, p.chips)
        attend(p, r, a, step, 2 * yy + 1 - c)
        if s == 1:
            out_ready()
        shares.give(s, branch(2 * yy + 1 - c))
        attend(p, r, a, step, 2 * yy + c)
        shares.pass_on(s, branch(2 * yy + c))
    after()
    attend(p, r, a, step, 2 * y)
    shares.give(0, branch(2 * y + 1 - c))
    total = shares.total(branch(b))
    gather.end()
    return total


def attention_grads(p, r, a, step, bb):
    cols, sub = p.cols, p.seq // QROWS
    table = pick_table(p, r, step, bb)
    weights = a.gates[bb, 0 : p.top, :]
    values = mm(r.wo[...], r.gt[bb])
    for k in range(sub):
        lanes = slice(k * QROWS, (k + 1) * QROWS)
        here = table[:, lanes]
        picked = pick_rows(p, here, lambda e: values[e * cols : (e + 1) * cols, lanes])
        grads = []
        for j in range(p.top):
            slot = slice(j * QROWS, (j + 1) * QROWS)
            products = picked[j] * a.att[bb * sub + k, :, slot].astype(F32)
            grads.append(jnp.sum(products, axis=0, keepdims=True))
            for head in range(p.heads):
                mean = jnp.sum(products[head * HD : (head + 1) * HD], axis=0, keepdims=True)
                r.means[bb * sub + k, head : head + 1, slot] = mean * weights[j : j + 1, lanes]
            a.att[bb * sub + k, :, slot] = (picked[j] * weights[j : j + 1, lanes]).astype(BF)
        mean = sum(weights[j : j + 1, lanes] * grads[j] for j in range(p.top))
        back = [weights[j : j + 1, lanes] * (grads[j] - mean) for j in range(p.top)]
        for e in range(p.mixers):
            r.dlog[bb, e : e + 1, lanes] = spread_rows(p, here, back, e)


def attend_back(p, r, a, step, bb):
    cols, sub = p.cols, p.seq // QROWS

    @pl.loop(0, sub)
    def _(k):
        i = bb * sub + k
        start = aligned(i * QROWS, QROWS)
        keys = pl.ds(start, WINDOW)
        bias = attention_mask(r, start)
        bias = jnp.concatenate([bias] * p.top, axis=1)
        queries = a.qs[i]
        grads = a.att[i]
        query_grads = []
        for head in range(p.heads):
            rows = slice(head * HD, (head + 1) * HD)
            scores = mm(r.k_heads[head, keys, :], queries) + bias
            probs = jnp.exp(scores - a.lse[i, head : head + 1, :])
            mean = r.means[i, head : head + 1, :]
            dscores = (probs * (mm(r.v_heads[head, keys, :], grads) - mean)).astype(BF)
            r.dvt[rows, keys] += mm_nt(grads[rows], probs.astype(BF))
            r.dkt[rows, keys] += mm_nt(queries[rows], dscores)
            query_grads.append(mm(a.kt[rows, keys], dscores) * (HD**-0.5))
        at = pl.ds(aligned(k * QROWS, QROWS), QROWS)
        table = r.all_picks[bb, 8 * step : 8 * step + p.top, at]
        merged = jnp.concatenate(query_grads, axis=0)
        values = [merged[:, j * QROWS : (j + 1) * QROWS] for j in range(p.top)]
        for e in range(p.mixers):
            r.dall[e * cols : (e + 1) * cols, pl.ds(start, QROWS)] = spread_rows(p, table, values, e).astype(BF)


def attention_backward(p, r, a, step, state, grad, before, middle, last):
    b, _ = place()
    y, c = b // 2, lax.rem(b, 2)
    r.gt[b] = grad.T.astype(BF)
    gather = PackGather(p, r.gt, a.back_gather_sems)
    gather.begin()
    r.dkt[...] = jnp.zeros_like(r.dkt)
    r.dvt[...] = jnp.zeros_like(r.dvt)
    before()

    @pl.loop(0, (p.length + MAXLEN) // QROWS)
    def _(k):
        at = pl.ds(aligned(k * QROWS, QROWS), QROWS)
        head_rows(p, r.k_heads, at, a.kt[:, at].astype(F32))
        head_rows(p, r.v_heads, at, a.vt[:, at].astype(F32))

    attention_grads(p, r, a, step, b)
    gather.finish_near()
    attention_grads(p, r, a, step, 2 * y + 1 - c)
    attend_back(p, r, a, step, 2 * y)
    gather.finish_far()
    for s in range(1, p.chips):
        yy = turn(y, s, p.chips)

        @pl.loop(0, 2)
        def _(k):
            attention_grads(p, r, a, step, 2 * yy + k)

    middle()
    for s in range(1, p.chips):
        yy = turn(y, s, p.chips)

        @pl.loop(0, 2)
        def _(k):
            attend_back(p, r, a, step, 2 * yy + k)

    cols = p.cols

    def branch(bb):
        lanes = pl.ds(aligned(bb * p.seq, p.seq), p.seq)
        past = pl.ds(aligned(bb * p.seq + MAXLEN, QROWS), p.seq)
        r.dall[p.mixers * cols : (p.mixers + 1) * cols, lanes] = r.dkt[:, past].astype(BF)
        r.dall[(p.mixers + 1) * cols :, lanes] = r.dvt[:, past].astype(BF)
        return mm(r.all_w[:, : p.qkv], r.dall[:, lanes]) + mm(r.router_col[...], r.dlog[bb].astype(BF))

    shares = PackSum(p, r, a.back_sum_sems)
    for s in range(1, p.chips):
        yy = turn(y, s, p.chips)
        shares.give(s, branch(2 * yy + 1 - c))
        shares.pass_on(s, branch(2 * yy + c))
    attend_back(p, r, a, step, 2 * y + 1)
    shares.give(0, branch(2 * y + 1 - c))
    own = branch(b)
    last()
    router = sum(mm_nt(r.dlog[bb].astype(BF), a.nt[bb]) for bb in range(p.blk))
    grad_n = shares.total(own).T
    gather.end()
    back, gain = norm_back(state, r.gain_one[...], grad_n)
    return grad + back, gain, router


def attention_weight_grads(p, r, a, start, stop, add):
    tile = 2 * p.cols
    for first in range(start, stop, tile):
        total = None
        for bb in range(p.blk):
            lanes = slice(bb * p.seq, (bb + 1) * p.seq)
            if first < p.qkv:
                term = mm_nt(a.nt[bb], r.dall[first : first + tile, lanes])
            else:
                term = mm_nt(r.gt[bb], a.mix[first - p.qkv : first - p.qkv + tile, lanes])
            total = term if total is None else total + term
        at = slice(first, first + tile)
        r.grad_w[:, at] = (r.grad_w[:, at].astype(F32) + total if add else total).astype(BF)


def own_lane(p):
    b, d = place()
    mine = d * p.local + b // p.group
    return jnp.where(lax.broadcasted_iota(jnp.int32, (1, LANES), 1) == mine, 1.0, 0.0)


def slot_gates(p, r, rows, pair):
    own = own_lane(p)
    logits = mm(rows, r.router[...])
    return 1.0 / (1.0 + jnp.exp(jnp.sum(logits * (pair - 2.0 * own), axis=-1, keepdims=True)))


def gelu_both(inner):
    half = 0.5 * (1.0 + lax.erf(inner * 0.7071067811865476))
    slope = half + inner * jnp.exp(-0.5 * inner * inner) * 0.3989422804014327
    return inner * half, slope


def slot_groups(p):
    per = max(1, p.experts // 4)
    return [(pl.ds(first * p.cap, per * p.cap), range(first, first + per)) for first in range(0, p.experts, per)]


def expert_output(p, r, rows, at, keep):
    total = None
    for start in range(0, p.ff, p.tile):
        lanes = slice(start, start + p.tile)
        inner = mm(rows, r.all_in[:, lanes])
        if keep:
            act, slope = gelu_both(inner)
            act = act.astype(BF)
            r.act[at, lanes] = act
            r.slope[at, lanes] = slope.astype(BF)
        else:
            act = (inner * (0.5 * (1.0 + lax.erf(inner * 0.7071067811865476)))).astype(BF)
        term = mm(act, r.all_back[lanes, :])
        total = term if total is None else total + term
    return total


def expert_keep(p, r, rows, at):
    for start in range(0, p.ff, p.tile):
        lanes = slice(start, start + p.tile)
        act, slope = gelu_both(mm(rows, r.all_in[:, lanes]))
        r.act[at, lanes] = act.astype(BF)
        r.slope[at, lanes] = slope.astype(BF)


def expert_input_grad(p, r, at, u, rows, out, pair, dst):
    gate = slot_gates(p, r, rows, pair)
    grads = (u * gate).astype(BF)
    r.u_in[at, :] = grads
    coeff = gate * (1.0 - gate) * jnp.sum(u * out, axis=-1, keepdims=True) * (2.0 * own_lane(p) - pair)
    coeff = coeff.astype(BF)
    r.coeff[at, :] = coeff
    dst[at, :] = mm_nt(coeff, r.router[...]).astype(BF)
    total = None
    for start in range(0, p.ff, p.tile):
        lanes = slice(start, start + p.tile)
        inner = (mm_nt(grads, r.all_back[lanes, :]) * r.slope[at, lanes].astype(F32)).astype(BF)
        r.slope[at, lanes] = inner
        term = mm_nt(inner, r.all_in[:, lanes])
        total = term if total is None else total + term
    dst[at, :] = (total + dst[at, :].astype(F32)).astype(BF)


def expert_weight_grads(p, r, arrived, add):
    r.arrived_t[...] = arrived[...].astype(F32).T.astype(BF)
    for start in range(0, p.ff, p.tile // 2):
        lanes = slice(start, start + p.tile // 2)
        term = mm(r.act[:, lanes].astype(F32).T.astype(BF), r.u_in[...])
        r.grad_back[lanes, :] = (r.grad_back[lanes, :].astype(F32) + term if add else term).astype(BF)
        term = mm(r.arrived_t[...], r.slope[:, lanes])
        r.grad_in[:, lanes] = (r.grad_in[:, lanes].astype(F32) + term if add else term).astype(BF)
    return mm(r.coeff[...].astype(F32).T.astype(BF)[0 : p.experts], arrived[...])


def slot_tables(p, r):
    b, d = place()
    e = b // p.group
    place_in = lax.broadcasted_iota(jnp.int32, (p.experts, 1), 0)
    ids = lax.rem(d + lax.rem(place_in, p.dp), p.dp) * p.local + lax.rem(e + place_in // p.dp, p.local)
    earlier = (
        lax.broadcasted_iota(jnp.int32, (p.seq, p.seq), 0) < lax.broadcasted_iota(jnp.int32, (p.seq, p.seq), 1)
    ).astype(BF)
    slot_ids = lax.broadcasted_iota(jnp.int32, (p.cap, p.seq), 0).astype(F32)
    lane_ids = lax.broadcasted_iota(jnp.int32, (LANES, 1), 0)
    copies = []
    for step in range(2):
        one = r.routes[8 * step + p.top : 8 * step + p.top + 1, :]
        two = r.routes[8 * step + p.top + 1 : 8 * step + p.top + 2, :]
        member = jnp.where((one == ids) | (two == ids), 1.0, 0.0)
        rank = jnp.where(member > 0.5, mm(member.astype(BF), earlier), -1.0)
        for s in range(p.experts):
            r.disp[step, pl.ds(s * p.cap, p.cap), :] = jnp.where(rank[s : s + 1, :] == slot_ids, 1.0, 0.0).astype(BF)
        table = r.disp[step]
        r.comb[step] = table.astype(F32).T.astype(BF)
        pair = jnp.where((one == lane_ids) | (two == lane_ids), 1.0, 0.0).astype(BF)
        r.pair_out[step] = mm_nt(table, pair).astype(BF)
        r.pair[step, 0 : p.cap, :] = r.pair_out[step, 0 : p.cap, :]
        for s in range(1, p.experts):
            rows = pl.ds(s * p.cap, p.cap)
            slot = step * p.experts + s
            copies.append(
                send(r.pair_out.at[step, rows], r.pair.at[step, rows], (r.pair_s, r.pair_r), slot, slot_peer(p, s))
            )
    return copies


def forward_kernel(p, r):
    b, d = place()
    z, x = d // p.lo, lax.rem(d, p.lo)
    e, g = b // p.group, lax.rem(b, p.group)
    own_rows = r.wall.shape[0]
    in_rows, back_rows = r.weight_in.shape[1], r.weight_back.shape[1]

    def w_at(index, part):
        lanes = slice(0, p.qkv) if part == 0 else slice(p.qkv, p.all_cols)
        return r.all_w.at[pl.ds(aligned(index * own_rows, own_rows), own_rows), lanes]

    def in_at(index):
        return r.all_in.at[pl.ds(aligned(index * in_rows, in_rows), in_rows)]

    def back_at(index):
        return r.all_back.at[pl.ds(aligned(index * back_rows, back_rows), back_rows)]

    greet(pack_peers(p) + slot_peers(p) + dp_peers(p) + expert_peers(p))
    r.all_w[pl.ds(aligned(d * own_rows, own_rows), own_rows), :] = r.wall[...]
    along, across = {}, {}

    def w_begin(part):
        own = w_at(d, part)
        for s in range(1, p.hi):
            k = part * (p.hi - 1) + s - 1
            along[part, s] = send(own, own, (r.hi_s, r.hi_r), k, (b, turn(z, s, p.hi) * p.lo + x))

    def w_cross(part, s):
        rows = w_at(turn(z, -s, p.hi) * p.lo + x, part)
        for t in range(1, p.lo):
            k = (part * p.hi + s) * (p.lo - 1) + t - 1
            across[part, s, t] = send(rows, rows, (r.lo_s, r.lo_r), k, (b, z * p.lo + turn(x, t, p.lo)))

    def w_finish(part):
        for s in range(p.hi):
            for t in range(1, p.lo):
                across[part, s, t].wait_recv()

    local, over, beside = [], {}, []

    def experts_begin():
        for s in range(1, p.local):
            to = turn(e, s, p.local)
            peer = (to * p.group + g, d)
            over[s, 0] = send(r.weight_in.at[to], in_at(b), (r.wide_s, r.wide_r), 2 * s - 2, peer)
            over[s, 1] = send(r.weight_back.at[to], back_at(b), (r.wide_s, r.wide_r), 2 * s - 1, peer)
        for t in range(1, p.group):
            peer = (e * p.group + turn(g, t, p.group), d)
            beside.append(send(r.weight_in.at[e], in_at(b), (r.near_s, r.near_r), 2 * t - 2, peer))
            beside.append(send(r.weight_back.at[e], back_at(b), (r.near_s, r.near_r), 2 * t - 1, peer))

    def experts_pass():
        for s in range(1, p.local):
            source = turn(e, -s, p.local) * p.group + g
            for which, rows in ((0, in_at(source)), (1, back_at(source))):
                over[s, which].wait_recv()
                for t in range(1, p.group):
                    k = (s * (p.group - 1) + t - 1) * 2 + which
                    peer = (e * p.group + turn(g, t, p.group), d)
                    beside.append(send(rows, rows, (r.near_s, r.near_r), k, peer))

    tables = []
    saves = []

    w_begin(0)
    w_cross(0, 0)
    r.all_picks[b] = r.routes[...]
    picks = PackGather(p, r.all_picks, r.picks_sems)
    picks.begin()
    state = r.x[...].astype(F32)

    def before(gather):
        local.extend(moves(r, [(r.weight_in.at[e], in_at(b)), (r.weight_back.at[e], back_at(b))]))
        segment_columns(p, r.segments, r.seg_cols)
        tables.extend(slot_tables(p, r))
        gather.finish_far()
        picks.finish_far()
        for s in range(1, p.hi):
            along[0, s].wait_recv()
            w_cross(0, s)
        w_begin(1)
        w_cross(1, 0)
        experts_begin()
        w_finish(0)
        transposed(r.w_t, r.all_w, p.qkv, 0, 2 * p.cols)

    def out_ready():
        for s in range(1, p.hi):
            along[1, s].wait_recv()
            w_cross(1, s)
        w_finish(1)

    def after():
        saves.extend(moves(r, [(r.all_w, r.all_w_out), (r.disp, r.disp_out), (r.comb, r.comb_out)]))
        experts_pass()

    total = attention_forward(p, r, r.a, 0, state, before, out_ready, after)
    middle = state + total.T
    r.middle[...] = middle
    m = (norm_parts(middle)[1] * r.gain_two[...]).astype(BF)
    r.outgoing[...] = mm(r.disp[0], m).astype(BF)
    there = slot_sends(p, r.outgoing, r.arrived, (r.go_s, r.go_r), slot_peer)
    saves.extend(moves(r, [(getattr(r.a, k), getattr(r, k + "_out")) for k in SAVED]))
    for copy in tables:
        copy.wait_recv()
    for copy in beside:
        copy.wait_recv()
    arrive(local)
    saves.extend(moves(r, [(r.all_in, r.all_in_out), (r.all_back, r.all_back_out), (r.pair, r.pair_end)]))
    back = {}
    for at, sources in slot_groups(p):
        receive(there, sources)
        rows = r.arrived[at, :]
        out = expert_output(p, r, rows, at, False)
        r.produced[at, :] = out.astype(BF)
        r.ret_out[at, :] = (out * slot_gates(p, r, rows, r.pair[0, at, :].astype(F32))).astype(BF)
        for s in sources:
            if s:
                back[s] = slot_send(p, r.ret_out, r.ret_in, (r.ret_s, r.ret_r), s, slot_source(p, s))
    r.ret_in[0 : p.cap, :] = r.ret_out[0 : p.cap, :]
    receive(back, range(p.experts))
    r.first[...] = r.middle[...] + mm(r.comb[0], r.ret_in[...])
    sent(there)
    sent(back)
    sent(tables)
    sent(beside)
    sent(along)
    sent(across)
    sent(over)
    picks.end()
    arrive(saves)


def turn_kernel(p, r):
    greet(pack_peers(p) + slot_peers(p))
    early = moves(r, [(r.all_w_in, r.all_w), (r.disp_in, r.disp), (r.comb_in, r.comb), (r.pair_in, r.pair)])
    weights = moves(r, [(r.all_in_in, r.all_in), (r.all_back_in, r.all_back)])
    first = r.first[...]
    stop = 1.0 / (1.0 + jnp.exp(-jnp.sum(first * r.halt[...], axis=-1, keepdims=True)))
    cot = r.cot[...].astype(F32)
    there_u, saves = {}, []

    def before(gather):
        arrive(early)
        r.u_out[...] = mm(r.disp[...], ((1.0 - stop) * cot).astype(BF)).astype(BF)
        there_u.update(slot_sends(p, r.u_out, r.u_in, (r.u_s, r.u_r), slot_peer))
        segment_columns(p, r.segments, r.seg_cols)
        transposed(r.w_t, r.all_w, p.qkv, 0, 2 * p.cols)

    total = attention_forward(p, r, r.a, 1, first, before, lambda: None, lambda: None)
    middle = first + total.T
    r.middle[...] = middle
    m = (norm_parts(middle)[1] * r.gain_two[...]).astype(BF)
    r.outgoing[...] = mm(r.disp[...], m).astype(BF)
    there = slot_sends(p, r.outgoing, r.arrived, (r.go_s, r.go_r), slot_peer)
    transposed(r.wo, r.all_w, p.mixers * p.cols, p.qkv, 2 * p.cols)
    arrive(weights)
    sent(there_u)
    ret_out = r.u_out
    back, back_out = {}, {}
    for at, sources in slot_groups(p):
        receive(there_u, sources)
        receive(there, sources)
        rows = r.arrived[at, :]
        pair = r.pair[at, :].astype(F32)
        out = expert_output(p, r, rows, at, True)
        ret_out[at, :] = (out * slot_gates(p, r, rows, pair)).astype(BF)
        expert_input_grad(p, r, at, r.u_in[at, :].astype(F32), rows, out, pair, r.gret_out)
        for s in sources:
            if s:
                back[s] = slot_send(p, r.gret_out, r.gret_in, (r.gret_s, r.gret_r), s, slot_source(p, s))
    r.gret_in[0 : p.cap, :] = r.gret_out[0 : p.cap, :]
    r.ret_in[0 : p.cap, :] = ret_out[0 : p.cap, :]
    r.grad_router[...] = expert_weight_grads(p, r, r.arrived, False)
    saves.extend(moves(r, [(r.grad_in, r.grad_in_out), (r.grad_back, r.grad_back_out)]))
    receive(back, range(p.experts))
    step_back, gain_two = norm_back(r.middle[...], r.gain_two[...], mm(r.comb[...], r.gret_in[...]))
    r.grad_gain_two[...] = gain_two
    grad_middle = (1.0 - stop) * cot + step_back

    def before_back():
        for s in range(1, p.experts):
            back_out[s] = slot_send(p, ret_out, r.ret_in, (r.ret_s, r.ret_r), s, slot_source(p, s))

    def last():
        attention_weight_grads(p, r, r.a, 0, p.all_cols, False)

    grad, gain_one, router = attention_backward(
        p, r, r.a, 1, first, grad_middle, before_back, lambda: None, last
    )
    saves.extend(moves(r, [(r.grad_w, r.grad_w_out)]))
    r.grad_gain_one[...] = gain_one
    r.grad_mixer[...] = router
    receive(back_out, range(p.experts))
    second = r.middle[...] + mm(r.comb[...], r.ret_in[...])
    r.result[...] = (stop * first + (1.0 - stop) * second).astype(BF)
    grad_stop = jnp.sum(cot * (first - second), axis=-1, keepdims=True)
    coeff = grad_stop * stop * (1.0 - stop)
    r.grad_halt[...] = jnp.sum(coeff * first, axis=0, keepdims=True)
    r.grad_first[...] = stop * cot + coeff * r.halt[...] + grad
    for copies in (there, back, back_out):
        sent(copies)
    arrive(saves)


def backward_kernel(p, r):
    b, d = place()
    z, x = d // p.lo, lax.rem(d, p.lo)
    y, c = b // 2, lax.rem(b, 2)
    e, g = b // p.group, lax.rem(b, p.group)
    rows = r.out_w.shape[0]
    in_rows, back_rows = r.out_in.shape[1], r.out_back.shape[1]
    greet(pack_peers(p) + slot_peers(p) + dp_peers(p) + expert_peers(p))
    early = moves(
        r,
        [
            (r.disp_in, r.disp),
            (r.pair_in, r.pair),
            (r.arrived_in, r.arrived),
            (r.all_in_in, r.all_in),
            (r.all_back_in, r.all_back),
            (r.produced_in, r.produced),
        ],
    )
    later = moves(
        r, [(r.grad_in_in, r.grad_in), (r.grad_back_in, r.grad_back), (r.comb_in, r.comb), (r.all_w_in, r.all_w)]
    )
    later += moves(r, [(r.grad_w_in, r.grad_w)])
    later += moves(r, [(getattr(r, k + "_in"), getattr(r.a, k)) for k in SAVED])
    grad_first = r.grad_first[...]
    arrive(early)
    r.u_out[...] = mm(r.disp[...], grad_first.astype(BF)).astype(BF)
    there = slot_sends(p, r.u_out, r.u_in, (r.u_s, r.u_r), slot_peer)
    for at, _ in slot_groups(p):
        expert_keep(p, r, r.arrived[at, :], at)
    segment_columns(p, r.segments, r.seg_cols)
    arrive(later)
    transposed(r.wo, r.all_w, p.mixers * p.cols, p.qkv, 2 * p.cols)
    back = {}
    for at, sources in slot_groups(p):
        receive(there, sources)
        pair = r.pair[at, :].astype(F32)
        out = r.produced[at, :].astype(F32)
        expert_input_grad(p, r, at, r.u_in[at, :].astype(F32), r.arrived[at, :], out, pair, r.produced)
        for s in sources:
            if s:
                back[s] = slot_send(p, r.produced, r.gret_in, (r.gret_s, r.gret_r), s, slot_source(p, s))
    r.gret_in[0 : p.cap, :] = r.produced[0 : p.cap, :]
    r.grad_router[...] = expert_weight_grads(p, r, r.arrived, True)

    def row_block(ref, index, size, lanes=slice(None)):
        return ref.at[pl.ds(aligned(index * size, size), size), lanes]

    near = {}
    for k in range(p.local):
        to = turn(e, k + 1, p.local)
        for t in range(1, p.group):
            member = turn(g, t, p.group)
            slot = k * (p.group - 1) + t - 1
            peer = (e * p.group + member, d)
            owner = to * p.group + member
            near[k, t, 0] = send(
                row_block(r.grad_in, owner, in_rows), r.in_near.at[slot], (r.near_s, r.near_r), 2 * slot, peer
            )
            near[k, t, 1] = send(
                row_block(r.grad_back, owner, back_rows), r.back_near.at[slot], (r.near_s, r.near_r), 2 * slot + 1, peer
            )
    receive(back, range(p.experts))
    step_back, gain_two = norm_back(r.middle[...], r.gain_two[...], mm(r.comb[...], r.gret_in[...]))
    grad_middle = grad_first + step_back
    wide, lo_copies, hi_copies = {}, {}, {}

    def experts_wide():
        for k in range(p.local):
            to = turn(e, k + 1, p.local)
            total_in = row_block(r.grad_in, to * p.group + g, in_rows)[...].astype(F32)
            total_back = row_block(r.grad_back, to * p.group + g, back_rows)[...].astype(F32)
            for t in range(1, p.group):
                slot = k * (p.group - 1) + t - 1
                near[k, t, 0].wait_recv()
                near[k, t, 1].wait_recv()
                total_in = total_in + r.in_near[slot].astype(F32)
                total_back = total_back + r.back_near[slot].astype(F32)
            if k < p.local - 1:
                r.in_far_out[k] = total_in.astype(BF)
                r.back_far_out[k] = total_back.astype(BF)
                peer = (to * p.group + g, d)
                wide[k, 0] = send(r.in_far_out.at[k], r.in_far.at[k], (r.wide_s, r.wide_r), 2 * k, peer)
                wide[k, 1] = send(r.back_far_out.at[k], r.back_far.at[k], (r.wide_s, r.wide_r), 2 * k + 1, peer)
            else:
                r.out_in[e] = total_in.astype(BF)
                r.out_back[e] = total_back.astype(BF)

    parts = (slice(0, p.qkv), slice(p.qkv, p.all_cols))

    def sum_begin(part):
        for k in range(p.hi):
            to = turn(z, k + 1, p.hi)
            for t in range(1, p.lo):
                slot = k * (p.lo - 1) + t - 1
                xx = turn(x, t, p.lo)
                lo_copies[part, k, t] = send(
                    row_block(r.grad_w, to * p.lo + xx, rows, parts[part]),
                    r.w_lo.at[slot, :, parts[part]],
                    (r.lo_s, r.lo_r),
                    part * p.hi * (p.lo - 1) + slot,
                    (b, z * p.lo + xx),
                )

    def sum_pass(part):
        lanes = parts[part]
        for k in range(p.hi):
            to = turn(z, k + 1, p.hi)
            total = row_block(r.grad_w, to * p.lo + x, rows, lanes)[...].astype(F32)
            for t in range(1, p.lo):
                lo_copies[part, k, t].wait_recv()
                total = total + r.w_lo[k * (p.lo - 1) + t - 1, :, lanes].astype(F32)
            if k < p.hi - 1:
                r.w_hi_out[k, :, lanes] = total.astype(BF)
                hi_copies[part, k] = send(
                    r.w_hi_out.at[k, :, lanes],
                    r.w_hi.at[k, :, lanes],
                    (r.hi_s, r.hi_r),
                    part * (p.hi - 1) + k,
                    (b, to * p.lo + x),
                )
            else:
                r.out_w[:, lanes] = total

    def sum_finish(part):
        lanes = parts[part]
        total = r.out_w[:, lanes]
        for k in range(p.hi - 1):
            hi_copies[part, k].wait_recv()
            total = total + r.w_hi[k, :, lanes].astype(F32)
        r.out_w[:, lanes] = total

    def middle():
        experts_wide()
        attention_weight_grads(p, r, r.a, p.qkv, p.all_cols, True)
        sum_begin(1)

    def last():
        sum_pass(1)
        attention_weight_grads(p, r, r.a, 0, p.qkv, True)
        sum_begin(0)

    grad, gain_one, router = attention_backward(
        p, r, r.a, 0, r.x[...].astype(F32), grad_middle, lambda: None, middle, last
    )
    sum_pass(0)
    r.input_grad[...] = grad.astype(BF)
    small = r.out_small
    small[...] = jnp.zeros_like(small)
    small[0:1, :] = r.gain_one_before[...] + gain_one
    small[1:2, :] = r.gain_two_before[...] + gain_two
    small[2:3, :] = r.halt_before[...]
    small[8 : 8 + p.mixers, :] = r.mixer_before[...] + router
    small[8 + p.mixers :, :] = r.router_before[...] + r.grad_router[...]
    current = small[...]
    tiny = []
    sem = base = 0
    axes = (
        (2, c, lambda t: (2 * y + turn(c, t, 2), d)),
        (p.chips, y, lambda t: (2 * turn(y, t, p.chips) + c, d)),
        (p.lo, x, lambda t: (b, z * p.lo + turn(x, t, p.lo))),
        (p.hi, z, lambda t: (b, turn(z, t, p.hi) * p.lo + x)),
    )
    for size, index, peer in axes:
        r.all_small[base + index] = current
        at = r.all_small.at[base + index]
        copies = []
        for t in range(1, size):
            copies.append(send(at, at, (r.tiny_s, r.tiny_r), sem, peer(t)))
            sem += 1
        for copy in copies:
            copy.wait_recv()
        current = r.all_small[base]
        for k in range(1, size):
            current = current + r.all_small[base + k]
        base += size
        tiny += copies
    r.out_small[...] = current
    for k in range(p.local - 1):
        source = turn(e, -(k + 1), p.local)
        wide[k, 0].wait_recv()
        wide[k, 1].wait_recv()
        r.out_in[source] = r.in_far[k]
        r.out_back[source] = r.back_far[k]
    sum_finish(1)
    sum_finish(0)
    for copies in (there, back, near, wide, lo_copies, hi_copies, tiny):
        sent(copies)


def output_kernel(p, r):
    cols = p.cols
    r.result_out[...] = r.result[...]
    r.input_grad_out[...] = r.input_grad[...]
    r.in_out[...] = r.out_in[...].astype(F32)
    r.back_out[...] = r.out_back[...].astype(F32)
    for e in range(p.mixers):
        r.query_out[e] = r.out_w[:, e * cols : (e + 1) * cols]
        start = p.qkv + e * cols
        r.out_out[e] = r.out_w[:, start : start + cols].T
    r.key_out[...] = r.out_w[:, p.mixers * cols : (p.mixers + 1) * cols]
    r.value_out[...] = r.out_w[:, (p.mixers + 1) * cols : p.qkv]
    r.gains_out[...] = r.small[0:8, :]
    r.routers_out[...] = r.small[8:, :].T


SAVED = ("nt", "qs", "kt", "vt", "lse", "att", "mix", "gates")


def dma(name, size):
    sem = pltpu.SemaphoreType.DMA((max(1, size),))
    return {name + "_s": sem, name + "_r": sem}


def pack_sems(p, name):
    sizes = (p.chips - 1, p.chips - 1, p.chips, p.chips)
    return {f"{name}_{k}": pltpu.SemaphoreType.DMA((max(1, size),)) for k, size in enumerate(sizes)}


def sum_scratch(p):
    far = max(1, p.chips - 1)
    return {
        "part": pltpu.VMEM((p.chips, p.width, p.seq), BF),
        "near_in": pltpu.VMEM((p.chips, p.width, p.seq), BF),
        "far_out": pltpu.VMEM((far, p.width, p.seq), BF),
        "far_in": pltpu.VMEM((far, p.width, p.seq), BF),
    }


def saved_shapes(p):
    return {
        "nt": ((p.blk, p.width, p.seq), BF),
        "qs": ((p.blocks, p.cols, p.top * QROWS), BF),
        "kt": ((p.cols, p.length + MAXLEN), BF),
        "vt": ((p.cols, p.length + MAXLEN), BF),
        "lse": ((p.blocks, 8, p.top * QROWS), F32),
        "att": ((p.blocks, p.cols, p.top * QROWS), BF),
        "mix": ((p.mixers * p.cols, p.length), BF),
        "gates": ((p.blk, 8, p.seq), F32),
    }


def launch(body, name, number, ins, outs, scratch):
    def spec(vmem):
        return pl.BlockSpec(memory_space=pltpu.VMEM if vmem else pl.ANY)

    names = list(ins) + list(outs) + list(scratch)

    def kernel(*refs):
        r = SimpleNamespace(**dict(zip(names, refs, strict=True)))
        r.moved = 0
        r.a = SimpleNamespace(**{k[2:]: v for k, v in vars(r).items() if k.startswith("a_")})
        for key in ("gather", "sum", "back_gather", "back_sum", "picks"):
            sems = [getattr(r, f"{key}_{k}") for k in range(4) if hasattr(r, f"{key}_{k}")]
            setattr(r.a, key + "_sems", sems)
            setattr(r, key + "_sems", sems)
        body(r)

    results = pl.pallas_call(
        kernel,
        out_shape=tuple(jax.ShapeDtypeStruct(shape, dtype) for shape, dtype, _ in outs.values()),
        in_specs=[spec(vmem) for _, vmem in ins.values()],
        out_specs=tuple(spec(vmem) for _, _, vmem in outs.values()),
        scratch_shapes=list(scratch.values()),
        compiler_params=pltpu.CompilerParams(
            collective_id=number, has_side_effects=number is not None, vmem_limit_bytes=VMEM_BYTES
        ),
        name=name,
    )(*[array for array, _ in ins.values()])
    return SimpleNamespace(**dict(zip(outs, results, strict=True)))


def on_device(
    inputs,
    segments,
    attention_routes,
    expert_routes,
    gain_mixer,
    gain_expert,
    weight_query,
    weight_key,
    weight_value,
    weight_out,
    router_mixer,
    router_expert,
    weight_in,
    weight_back,
    halt_weight,
    cotangent,
):
    blk, dp = lax.axis_size("blk"), lax.axis_size("dp")
    seq, width = inputs.shape[1:]
    experts, local = router_expert.shape[1], weight_in.shape[0]
    slots_of = max(2, 3 * seq // experts)
    hi = 4
    p = Plan(
        blk=blk,
        dp=dp,
        lo=dp // hi,
        hi=hi,
        seq=seq,
        width=width,
        heads=HEADS // blk,
        mixers=weight_query.shape[0],
        top=attention_routes.shape[-1],
        experts=experts,
        local=local,
        group=blk // local,
        cap=-(-slots_of // 16) * 16,
        ff=weight_in.shape[2],
    )
    cols, length, top = p.cols, p.length, p.top
    share, in_rows, back_rows = weight_key.shape[0], weight_in.shape[1], weight_back.shape[1]

    wall = jnp.concatenate(
        [
            jnp.transpose(weight_query, (1, 0, 2)).reshape(share, p.mixers * cols),
            weight_key,
            weight_value,
            jnp.transpose(weight_out, (2, 0, 1)).reshape(share, p.mixers * cols),
        ],
        axis=1,
    )
    routes = jnp.concatenate(
        [attention_routes[:, 0], expert_routes[:, 0], jnp.zeros((2, seq, 8 - top - expert_routes.shape[-1]), jnp.int32)],
        axis=-1,
    )
    routes = jnp.transpose(routes, (0, 2, 1)).reshape(16, seq)
    gain_one = gain_mixer.astype(F32).reshape(1, width)
    gain_two = gain_expert.astype(F32).reshape(1, width)
    halt = halt_weight.astype(F32).reshape(1, width)
    router_row = router_mixer.T
    router = jnp.pad(router_expert, ((0, 0), (0, LANES - experts)))

    slots_bf = pltpu.VMEM((p.slots, width), BF)
    saved = saved_shapes(p)
    attention_scratch = {
        "seg_cols": pltpu.VMEM((length + MAXLEN, 8), F32),
        "k_heads": pltpu.VMEM((p.heads, length + MAXLEN, cols), BF),
        "all_w": pltpu.VMEM((width, p.all_cols), BF),
        **{"a_" + k: pltpu.VMEM(*v) for k, v in saved.items()},
    }
    forward_scratch = {
        "w_t": pltpu.VMEM((p.qkv, width), BF),
        **pack_sems(p, "gather"),
        **pack_sems(p, "sum"),
        **sum_scratch(p),
    }
    backward_scratch = {
        "gt": pltpu.VMEM((blk, width, seq), BF),
        "v_heads": pltpu.VMEM((p.heads, length + MAXLEN, cols), BF),
        "means": pltpu.VMEM((p.blocks, 8, top * QROWS), F32),
        "dlog": pltpu.VMEM((blk, p.mixers, seq), F32),
        "dkt": pltpu.VMEM((cols, length + MAXLEN), F32),
        "dvt": pltpu.VMEM((cols, length + MAXLEN), F32),
        "dall": pltpu.VMEM((p.qkv, length), BF),
        "grad_w": pltpu.VMEM((width, p.all_cols), BF),
        **pack_sems(p, "back_gather"),
        **pack_sems(p, "back_sum"),
        **sum_scratch(p),
    }
    expert_scratch = {
        "all_in": pltpu.VMEM((width, p.ff), BF),
        "all_back": pltpu.VMEM((p.ff, width), BF),
    }
    expert_back_scratch = {
        "act": pltpu.VMEM((p.slots, p.ff), BF),
        "slope": pltpu.VMEM((p.slots, p.ff), BF),
        "coeff": pltpu.VMEM((p.slots, LANES), BF),
        "arrived_t": pltpu.VMEM((width, p.slots), BF),
        "u_out": slots_bf,
        "u_in": slots_bf,
        "gret_in": slots_bf,
        "grad_in": pltpu.VMEM((width, p.ff), BF),
        "grad_back": pltpu.VMEM((p.ff, width), BF),
        **dma("u", p.experts),
        **dma("gret", p.experts),
    }

    one = launch(
        functools.partial(forward_kernel, p),
        "forward",
        0,
        {
            "x": (inputs[0], True),
            "segments": (segments, True),
            "routes": (routes, True),
            "gain_one": (gain_one, True),
            "gain_two": (gain_two, True),
            "router_row": (router_row, True),
            "router": (router, True),
            "wall": (wall, True),
            "weight_in": (weight_in, False),
            "weight_back": (weight_back, False),
        },
        {
            "first": ((seq, width), F32, True),
            "middle": ((seq, width), F32, True),
            "arrived": ((p.slots, width), BF, True),
            "produced": ((p.slots, width), BF, True),
            "all_picks": ((blk, 16, seq), jnp.int32, True),
            "disp_out": ((2, p.slots, seq), BF, False),
            "comb_out": ((2, seq, p.slots), BF, False),
            "pair_end": ((2, p.slots, LANES), BF, False),
            "all_w_out": ((width, p.all_cols), BF, False),
            "all_in_out": ((width, p.ff), BF, False),
            "all_back_out": ((p.ff, width), BF, False),
            **{k + "_out": (*v, False) for k, v in saved.items()},
        },
        {
            **attention_scratch,
            **forward_scratch,
            **expert_scratch,
            "disp": pltpu.VMEM((2, p.slots, seq), BF),
            "comb": pltpu.VMEM((2, seq, p.slots), BF),
            "pair": pltpu.VMEM((2, p.slots, LANES), BF),
            "pair_out": pltpu.VMEM((2, p.slots, LANES), BF),
            "outgoing": slots_bf,
            "ret_out": slots_bf,
            "ret_in": slots_bf,
            **pack_sems(p, "picks"),
            **dma("hi", 2 * (p.hi - 1)),
            **dma("lo", 2 * p.hi * (p.lo - 1)),
            **dma("wide", 2 * (p.local - 1)),
            **dma("near", 2 * p.local * (p.group - 1)),
            **dma("pair", 2 * p.experts),
            **dma("go", p.experts),
            **dma("ret", p.experts),
            "moves": pltpu.SemaphoreType.DMA((16,)),
        },
    )
    two = launch(
        functools.partial(turn_kernel, p),
        "turn",
        1,
        {
            "first": (one.first, True),
            "cot": (cotangent[0], True),
            "halt": (halt, True),
            "segments": (segments, True),
            "all_picks": (one.all_picks, True),
            "gain_one": (gain_one, True),
            "gain_two": (gain_two, True),
            "router_row": (router_row, True),
            "router_col": (router_mixer, True),
            "router": (router, True),
            "disp_in": (one.disp_out[1], False),
            "comb_in": (one.comb_out[1], False),
            "pair_in": (one.pair_end[1], False),
            "all_w_in": (one.all_w_out, False),
            "all_in_in": (one.all_in_out, False),
            "all_back_in": (one.all_back_out, False),
        },
        {
            "result": ((seq, width), BF, True),
            "grad_first": ((seq, width), F32, True),
            "grad_halt": ((1, width), F32, True),
            "grad_gain_one": ((1, width), F32, True),
            "grad_gain_two": ((1, width), F32, True),
            "grad_mixer": ((p.mixers, width), F32, True),
            "grad_router": ((experts, width), F32, True),
            "grad_in_out": ((width, p.ff), BF, False),
            "grad_back_out": ((p.ff, width), BF, False),
            "grad_w_out": ((width, p.all_cols), BF, False),
        },
        {
            **attention_scratch,
            **forward_scratch,
            **backward_scratch,
            **expert_scratch,
            **expert_back_scratch,
            "wo": pltpu.VMEM((p.mixers * cols, width), BF),
            "disp": pltpu.VMEM((p.slots, seq), BF),
            "comb": pltpu.VMEM((seq, p.slots), BF),
            "pair": pltpu.VMEM((p.slots, LANES), BF),
            "middle": pltpu.VMEM((seq, width), F32),
            "outgoing": slots_bf,
            "arrived": slots_bf,
            "gret_out": slots_bf,
            "ret_in": slots_bf,
            **dma("go", p.experts),
            **dma("ret", p.experts),
            "moves": pltpu.SemaphoreType.DMA((16,)),
        },
    )
    near, far = p.local * (p.group - 1), max(1, p.local - 1)
    small_rows = 8 + p.mixers + experts
    three = launch(
        functools.partial(backward_kernel, p),
        "backward",
        2,
        {
            "x": (inputs[0], True),
            "grad_first": (two.grad_first, True),
            "middle": (one.middle, True),
            "segments": (segments, True),
            "all_picks": (one.all_picks, True),
            "gain_one": (gain_one, True),
            "gain_two": (gain_two, True),
            "router_col": (router_mixer, True),
            "router": (router, True),
            "halt_before": (two.grad_halt, True),
            "gain_one_before": (two.grad_gain_one, True),
            "gain_two_before": (two.grad_gain_two, True),
            "mixer_before": (two.grad_mixer, True),
            "router_before": (two.grad_router, True),
            "disp_in": (one.disp_out[0], False),
            "comb_in": (one.comb_out[0], False),
            "pair_in": (one.pair_end[0], False),
            "arrived_in": (one.arrived, False),
            "produced_in": (one.produced, False),
            "all_w_in": (one.all_w_out, False),
            "all_in_in": (one.all_in_out, False),
            "all_back_in": (one.all_back_out, False),
            "grad_in_in": (two.grad_in_out, False),
            "grad_back_in": (two.grad_back_out, False),
            "grad_w_in": (two.grad_w_out, False),
            **{k + "_in": (getattr(one, k + "_out"), False) for k in SAVED},
        },
        {
            "input_grad": ((seq, width), BF, True),
            "out_w": ((share, p.all_cols), F32, True),
            "out_in": ((local, in_rows, p.ff), BF, True),
            "out_back": ((local, back_rows, width), BF, True),
            "out_small": ((small_rows, width), F32, True),
        },
        {
            **attention_scratch,
            **backward_scratch,
            **expert_scratch,
            **expert_back_scratch,
            "wo": pltpu.VMEM((p.mixers * cols, width), BF),
            "disp": pltpu.VMEM((p.slots, seq), BF),
            "comb": pltpu.VMEM((seq, p.slots), BF),
            "pair": pltpu.VMEM((p.slots, LANES), BF),
            "arrived": slots_bf,
            "produced": slots_bf,
            "in_near": pltpu.VMEM((near, in_rows, p.ff), BF),
            "back_near": pltpu.VMEM((near, back_rows, width), BF),
            "in_far_out": pltpu.VMEM((far, in_rows, p.ff), BF),
            "in_far": pltpu.VMEM((far, in_rows, p.ff), BF),
            "back_far_out": pltpu.VMEM((far, back_rows, width), BF),
            "back_far": pltpu.VMEM((far, back_rows, width), BF),
            "w_lo": pltpu.VMEM((hi * (p.lo - 1), share, p.all_cols), BF),
            "w_hi_out": pltpu.VMEM((hi - 1, share, p.all_cols), BF),
            "w_hi": pltpu.VMEM((hi - 1, share, p.all_cols), BF),
            "grad_router": pltpu.VMEM((experts, width), F32),
            "all_small": pltpu.VMEM((2 + p.chips + p.lo + hi, small_rows, width), F32),
            **dma("near", 2 * near),
            **dma("wide", 2 * (local - 1)),
            **dma("lo", 2 * hi * (p.lo - 1)),
            **dma("hi", 2 * (hi - 1)),
            **dma("tiny", 2 + p.chips + p.lo + hi),
            "moves": pltpu.SemaphoreType.DMA((24,)),
        },
    )
    four = launch(
        functools.partial(output_kernel, p),
        "outputs",
        None,
        {
            "result": (two.result, True),
            "input_grad": (three.input_grad, True),
            "out_w": (three.out_w, True),
            "out_in": (three.out_in, True),
            "out_back": (three.out_back, True),
            "small": (three.out_small, True),
        },
        {
            "result_out": ((seq, width), BF, True),
            "input_grad_out": ((seq, width), BF, True),
            "query_out": (weight_query.shape, F32, True),
            "key_out": (weight_key.shape, F32, True),
            "value_out": (weight_value.shape, F32, True),
            "out_out": (weight_out.shape, F32, True),
            "in_out": (weight_in.shape, F32, True),
            "back_out": (weight_back.shape, F32, True),
            "gains_out": ((8, width), F32, True),
            "routers_out": ((width, p.mixers + experts), F32, True),
        },
        {},
    )
    return (
        four.result_out[None],
        four.input_grad_out[None],
        four.gains_out[0],
        four.gains_out[1],
        four.query_out,
        four.key_out,
        four.value_out,
        four.out_out,
        four.routers_out[:, : p.mixers],
        four.routers_out[:, p.mixers :],
        four.in_out,
        four.back_out,
        four.gains_out[2],
    )


def solution(mesh):
    return jax.shard_map(
        on_device,
        mesh=mesh,
        in_specs=(
            P("dp", "blk", None),
            P("dp", None),
            P(None, "dp", "blk", None),
            P(None, "dp", "blk", None),
            P(),
            P(),
            P(None, "dp", "blk"),
            P("dp", "blk"),
            P("dp", "blk"),
            P(None, "blk", "dp"),
            P(),
            P(),
            P("dp", "blk", None),
            P("dp", "blk", None),
            P(),
            P("dp", "blk", None),
        ),
        out_specs=(
            P("dp", "blk", None),
            P("dp", "blk", None),
            P(),
            P(),
            P(None, "dp", "blk"),
            P("dp", "blk"),
            P("dp", "blk"),
            P(None, "blk", "dp"),
            P(),
            P(),
            P("dp", "blk", None),
            P("dp", "blk", None),
            P(),
        ),
        check_vma=False,
    )
```

time: 1180 us -> 339 us (0.29)
  waiting for transfers between devices: 452 us -> 0 us
  Pallas kernels: 0 us -> 312 us
  matrix products: 255 us -> 0 us
  blocking collectives: 186 us -> 0 us
  local copies, waits for them, and re-layouts: 149 us -> 13.9 us
  other arithmetic: 75 us -> 5.96 us
  starting transfers between devices: 40.1 us -> 0 us
  between operations: 17.5 us -> 1.19 us
    pallas_call x0 -> x4, Pallas kernels: none -> 312 us  [launch(): pl.pallas_call(kernel, out_shape=tuple((jax.ShapeDtypeStruct(shape, dtype...]
    reduce_scatter x6 -> x0, waiting for transfers between devices: 271 us -> none  [the longest x1 78 us: on_device(): lax.psum_scatter(grad_query_w.astype(jnp.bfloat16), 'dp', scatter_dimensi...]
    dot_general x82 -> x0, matrix products: 255 us -> none  [the longest x2 34.6 us: step_forward(): jnp.einsum('sxcd,xdf->sxcf', arrived, local_in, preferred_element_type=jn...]
    all_gather x6 -> x0, blocking collectives: 96.7 us -> none  [the longest x1 33.6 us: on_device(): lax.all_gather(full_key, 'dp', axis=0, tiled=True)]
    all_to_all x6 -> x0, waiting for transfers between devices: 68.8 us -> none  [the longest x2 31.6 us: step_forward(): lax.all_to_all(produced, 'dp', split_axis=0, concat_axis=0, tiled=True)]
    all_gather x4 -> x0, waiting for transfers between devices: 65.9 us -> none  [the longest x1 25.7 us: on_device(): lax.all_gather(full_out, 'dp', axis=2, tiled=True)]
    all_to_all x2 -> x0, blocking collectives: 46.8 us -> none  [the longest x1 23.6 us: step_backward(): lax.all_to_all(grad_outgoing, 'dp', split_axis=0, concat_axis=0, tiled=True)]
    unnamed x440 -> x15, local copies, waits for them, and re-layouts: 50.9 us -> 5.97 us
  transfers between devices with their start and end apart: 28 -> 0, of which waited for: 17 -> 0; matrix products, arithmetic and copies ran while one was open for 23% -> 0% of each run, Pallas kernels for 0% -> 0%
where the time goes in v2:
time: 339 us; the launch traced here: 333 us
  Pallas kernels  312 us (92%)
  local copies, waits for them, and re-layouts  13.9 us (4%)
  other arithmetic  5.96 us (2%)
    pallas_call x4, Pallas kernels, launch(): pl.pallas_call(kernel, out_shape=tuple((jax.ShapeDtypeStruct(shape, dtype...  312 us

profile of v2, /device:TPU:0, one launch (start us, length us, event | category | flops | bytes accessed | tf_op | source)
XLA Modules:
  0.0 332.8 jit_solution(991713720361518769)
XLA Ops:
  0.6 0.0 copy-start
  0.7 0.1 pad.11.clone
  0.7 1.4 add_bitcast_fusion.refs_2_
  2.1 1.3 reshape.59
  3.4 1.3 reshape.61
  4.6 0.8 copy.29
  5.5 0.0 copy-start.4
  5.5 0.7 pad.4.refs_6_.refs_9_.refs_8_
  6.2 0.9 copy_bitcast_fusion
  7.1 1.5 pad_maximum_fusion.refs_7_
  8.6 100.7 %forward.1 = (f32[256,512]{1,0:T(8,128)}, f32[256,512]{1,0:T(8,128)}, bf16[768,512]{1,0:T(8,128)(2,1)}, bf16[768,512]{1,0:T(8,128)(2,1)}, s32[4,16,256]{2,1,0:T(...) custom-call(bf16[256,512]{1,0:T(8,128)(2,1)} %bitcast.42, ...), custom_call_target="tpu_custom_call" | custom-call | tf_op jit(solution)/shard_map/forward/pallas_call | solution.py:1129
  109.4 0.6 reshape.63
  109.9 0.8 copy.32.refs_8_.refs_7_
  110.7 2.0 slice_bitcast_fusion.1
  112.8 0.9 slice_bitcast_fusion
  113.7 0.8 slice_bitcast_fusion.4
  114.5 99.1 %turn.1 = (bf16[256,512]{1,0:T(8,128)(2,1)}, f32[256,512]{1,0:T(8,128)}, f32[1,512]{1,0:T(1,128)}, f32[1,512]{1,0:T(1,128)}, f32[1,512]{1,0:T(1,128)}, /*index=5...) custom-call(f32[256,512]{1,0:T(8,128)} %get-tuple-element.57.refs_0_, ...), custom_call_target="tpu_custom_call" | custom-call | tf_op jit(solution)/shard_map/turn/pallas_call | solution.py:1129
  213.6 107.3 %backward.1 = (bf16[256,512]{1,0:T(8,128)(2,1)}, f32[64,2304]{1,0:T(8,128)}, bf16[2,128,2048]{2,1,0:T(8,128)(2,1)}, bf16[2,512,512]{2,1,0:T(8,128)(2,1)}, f32[32,512]{1,0:T(8,128)}) custom-call(bf16[256,512]{1,0:T(8,128)(2,1)} %bitcast.43, f32[256,512]{1,0:T(8,128)} %get-tuple-element.66.refs_1_, f32[256,512]{1,0:T(8,128)} %get-tuple-element.67.refs_2_, ...), custom_call_target="tpu_custom_call" | custom-call | tf_op jit(solution)/shard_map/backward/pallas_call | solution.py:1129
  320.9 4.7 %outputs.1 = (bf16[256,512]{1,0:T(8,128)(2,1)}, bf16[256,512]{1,0:T(8,128)(2,1)}, f32[8,64,128]{2,1,0:T(8,128)}, f32[64,128]{1,0:T(8,128)}, f32[64,128]{1,0:T(8,...) custom-call(bf16[256,512]{1,0:T(8,128)(2,1)} %get-tuple-element.65.r, ...), custom_call_target="tpu_custom_call" | custom-call | tf_op jit(solution)/shard_map/outputs/pallas_call | solution.py:1129
  325.6 1.4 fusion
  327.0 1.9 copy.34
  328.9 1.7 copy.35
  330.6 1.1 slice.42
  331.7 0.7 copy.36
  (9 shorter events, 0.0 us)
Async XLA Ops:
  0.6 5.6 %copy-start = (bf16[8,64,128]{2,1,0:T(8,128)(2,1)S(1)}, bf16[8,64,128]{2,1,0:T(8,128)(2,1)}, u32[]{:S(2)}) copy-start(bf16[8,64,128]{2,1,0:T(8,128)(2,1)} %param.22) | copy-start | bytes 393220
  5.5 103.9 %copy-start.4 = (bf16[512]{0:T(512)(128)(2,1)S(1)}, bf16[512]{0:T(512)(128)(2,1)}, u32[]{:S(2)}) copy-start(bf16[512]{0:T(512)(128)(2,1)} %param.30) | copy-start | bytes 3076
  5.5 104.4 %copy-start.3 = (bf16[512,8]{0,1:T(8,128)(2,1)S(1)}, bf16[512,8]{0,1:T(8,128)(2,1)}, u32[]{:S(2)}) copy-start(bf16[512,8]{0,1:T(8,128)(2,1)} %param.26) | copy-start | bytes 24580
  109.3 3.4 %copy-start.1 = (bf16[2,256,768]{2,1,0:T(8,128)(2,1)S(1)}, bf16[2,256,768]{2,1,0:T(8,128)(2,1)}, u32[]{:S(2)}) copy-start(bf16[2,256,768]{2,1,0:T(8,128)(2,1)} %get-tuple-element.60) | copy-start | bytes 2359300
  109.3 4.4 %copy-start.2 = (bf16[2,768,128]{2,1,0:T(8,128)(2,1)S(1)}, bf16[2,768,128]{2,1,0:T(8,128)(2,1)}, u32[]{:S(2)}) copy-start(bf16[2,768,128]{2,1,0:T(8,128)(2,1)} %get-tuple-element.61) | copy-start | bytes 1179652
